TPU v7x, 32 devices: a whole 2x2x4 slice. The times are simulated.
32 devices in a mesh: gx: 4 (over y, x), gy: 4 (over z), gz: 2 (over core).
Axes of the slice: x: 2, y: 2, z: 4, core: 2. Of those that a mesh axis runs over, the one named last changes fastest.
Arguments:
- potential: float32 [64, 64, 1024], P('gz', 'gx', 'gy'), may hold values from -4 to 4
- charge: float32 [64, 64, 1024], P('gz', 'gx', 'gy'), may hold values from -6 to 6
- permittivity: float32 [64, 64, 1024], P('gz', 'gx', 'gy'), may hold values from 2 to 80
- labels: int32 [64, 64, 1024], P('gz', 'gx', 'gy'), may hold values from 0 to 2
- pattern: int32 [16, 16, 4, 2], P('gz', 'gx', 'gy'), may hold values from 0 to 127
- blocks: float32 [16, 16, 4, 2, 64, 64], P('gz', 'gx', 'gy'), may hold values from -0.5 to 0.5
Outputs:
- potential_next: float32 [64, 64, 1024], P('gz', 'gx', 'gy')
- coarse_correction: float32 [16, 16, 4, 64], P('gz', 'gx', 'gy')
All inputs are finite; a program needn't handle non-finite values.
Results may differ from a plain program's by a relative error of at most 0.00011.
Values sent between devices are 32-bit elements; how exact they have to be, the bound alone decides.
A program may use at most 64 MiB of HBM per device.

v0:
```python
import jax
import jax.numpy as jnp
from jax import lax
from jax.sharding import PartitionSpec as P

OMEGA = 0.8
CHARGE_SCALE = 40.0
COARSE_SCALE = 4.0


def padded_2(block, sides, width):
    for axis, dim in sides:
        count = lax.axis_size(axis)
        forward = [(i, i + 1) for i in range(count - 1)]
        backward = [(target, source) for source, target in forward]
        low = lax.ppermute(
            lax.slice_in_dim(block, block.shape[dim] - width, None, axis=dim), axis, forward
        )
        high = lax.ppermute(lax.slice_in_dim(block, 0, width, axis=dim), axis, backward)
        block = jnp.concatenate([low, block, high], axis=dim)
    return block


def screening_of(labels, permittivity):
    factor = jnp.where(labels == 1, 0.05, jnp.where(labels == 2, 0.2, 0.0))
    return factor * permittivity


def neighbours(padded):
    return (
        padded[2:, 1:-1, 1:-1],
        padded[:-2, 1:-1, 1:-1],
        padded[1:-1, 2:, 1:-1],
        padded[1:-1, :-2, 1:-1],
        padded[1:-1, 1:-1, 2:],
        padded[1:-1, 1:-1, :-2],
    )


def stencil(pad_pot, pad_perm):
    centre_pot = pad_pot[1:-1, 1:-1, 1:-1]
    centre_perm = pad_perm[1:-1, 1:-1, 1:-1]
    net_flux = jnp.zeros_like(centre_pot)
    face_sum = jnp.zeros_like(centre_pot)
    for near_pot, near_perm in zip(neighbours(pad_pot), neighbours(pad_perm)):
        coupling = 0.5 * (centre_perm + near_perm)
        net_flux = net_flux + coupling * (centre_pot - near_pot)
        face_sum = face_sum + coupling
    return (net_flux, face_sum)


def block_product(blocks, picked):
    return jnp.einsum("zxjkab,zxjkb->zxja", blocks, picked, precision=lax.Precision.HIGHEST)


def per_device(potential, charge, permittivity, labels, pattern, blocks):
    screening = screening_of(labels, permittivity)
    source = CHARGE_SCALE * charge
    cells_z, cells_x, cells_y = potential.shape
    padded = padded_2(jnp.stack([potential, permittivity]), (("gx", 2), ("gy", 3), ("gz", 1)), 1)
    pad_perm = padded[1]
    net_flux, face_sum = stencil(padded[0], pad_perm)
    diagonal = face_sum + screening * jnp.cosh(potential)
    swept = potential + OMEGA * (source - net_flux - screening * jnp.sinh(potential)) / diagonal
    pad_swept = padded_2(swept, (("gx", 1), ("gy", 2), ("gz", 0)), 1)
    swept_flux, unused = stencil(pad_swept, pad_perm)
    residual = source - swept_flux - screening * jnp.sinh(swept)
    agg_size = blocks.shape[-1]
    coarse_z = cells_z // 4
    coarse_x = cells_x // 4
    y_aggs = cells_y // (4 * agg_size)
    coarse_resid = (
        residual.reshape(coarse_z, 4, coarse_x, 4, y_aggs, agg_size, 4).sum(axis=(1, 3, 6)) / 64.0
    )
    coarse_diag = (
        diagonal.reshape(coarse_z, 4, coarse_x, 4, y_aggs, agg_size, 4).sum(axis=(1, 3, 6)) / 64.0
    )
    resid_xfirst = jnp.transpose(coarse_resid, (1, 0, 2, 3))
    yagg_rows = jnp.arange(y_aggs)[None, None, :, None]
    gathered = lax.all_gather(resid_xfirst, "gx", axis=0, tiled=True)
    column = jnp.transpose(gathered.reshape(-1, y_aggs, agg_size), (1, 0, 2))
    picked = column[yagg_rows, pattern]
    coupled = block_product(blocks, picked)
    correction = COARSE_SCALE * (coarse_resid + coupled) / coarse_diag
    spread = jnp.broadcast_to(
        correction[:, None, :, None, :, :, None], (coarse_z, 4, coarse_x, 4, y_aggs, agg_size, 4)
    ).reshape(cells_z, cells_x, cells_y)
    return (swept + spread, correction)


def solution(mesh):
    return jax.shard_map(
        per_device,
        mesh=mesh,
        in_specs=(
            P("gz", "gx", "gy"),
            P("gz", "gx", "gy"),
            P("gz", "gx", "gy"),
            P("gz", "gx", "gy"),
            P("gz", "gx", "gy", None),
            P("gz", "gx", "gy", None, None, None),
        ),
        out_specs=(P("gz", "gx", "gy"), P("gz", "gx", "gy", None)),
        check_vma=False,
    )
```

profile of v0, /device:TPU:0, one launch (start us, length us, event | category | flops | bytes accessed | tf_op | source)
XLA Modules:
  0.0 168.1 jit_solution(6385287187007189910)
XLA Ops:
  0.6 1.4 pad_maximum_fusion.28
  2.1 4.8 %collective-permute-start = (f32[2,32,1,256]{3,2,1,0:T(1,128)S(1)}, f32[2,32,1,256]{3,2,1,0:T(1,128)S(1)}, u32[]{:S(2)}, u32[]{:S(2)}) collective-permute-start(f32[2,32,1,256]{3,2,1,0:T(1,128)S(1)} %get-tuple-element.14), channel_id=1, source_target_pairs={{0,8},{8,16},{16,24},{1,9},{9,17},{17,25},{2,10},{10,18},{18,26},{... | collective-permute-start | bytes 196616 | tf_op jit(solution)/shard_map/ppermute | solution.py:16
  6.9 1.3 collective-permute-start.1
  8.8 4.3 %collective-permute-done.1 = f32[2,32,1,256]{3,2,1,0:T(1,128)S(1)} collective-permute-done((f32[2,32,1,256]{3,2,1,0:T(1,128)S(1)}, f32[2,32,1,256]{3,2,1,0:T(1,128)S(1)}, u32[]{:S(2)}, u32[]{:S(2)}) %collective-permute-start.1) | collective-permute-done | bytes 65568 | tf_op jit(solution)/shard_map/ppermute | solution.py:19
  13.1 1.4 pad_maximum_fusion.1
  14.5 1.4 fusion.52
  15.9 1.5 copy.22
  17.4 3.5 %collective-permute-start.2 = (f32[2,32,18,1]{1,0,3,2:T(2,128)S(1)}, f32[2,32,18,1]{1,0,3,2:T(2,128)S(1)}, u32[]{:S(2)}, u32[]{:S(2)}) collective-permute-start(f32[2,32,18,1]{1,0,3,2:T(2,128)S(1)} %copy.22), channel_id=1, source_target_pairs={{0,2},{2,4},{4,6},{1,3},{3,5},{5,7},{8,10},{10,12},{12,14},{9,11},... | collective-permute-start | bytes 13832 | tf_op jit(solution)/shard_map/ppermute | solution.py:16
  20.9 1.4 copy.23
  22.3 1.4 collective-permute-start.3
  23.8 1.3 copy.24
  25.1 3.0 %collective-permute-done.3 = f32[2,32,18,1]{1,0,3,2:T(2,128)S(1)} collective-permute-done((f32[2,32,18,1]{1,0,3,2:T(2,128)S(1)}, f32[2,32,18,1]{1,0,3,2:T(2,128)S(1)}, u32[]{:S(2)}, u32[]{:S(2)}) %collective-permute-start.3) | collective-permute-done | bytes 4640 | tf_op jit(solution)/shard_map/ppermute | solution.py:19
  30.4 1.3 collective-permute-start.4
  33.1 1.8 %collective-permute-done.5 = f32[2,1,18,258]{3,2,1,0:T(8,128)S(1)} collective-permute-done((f32[2,1,18,258]{3,2,1,0:T(8,128)S(1)}, f32[2,1,18,258]{3,2,1,0:T(8,128)S(1)}, u32[]{:S(2)}, u32[]{:S(2)}) %collective-permute-start.5) | collective-permute-done | bytes 37184 | tf_op jit(solution)/shard_map/ppermute | solution.py:19
  34.9 1.4 pad_maximum_fusion
  37.8 1.9 %fusion.48 = f32[32,16,256]{2,1,0:T(8,128)S(1)} fusion(f32[32,16,256]{2,1,0:T(8,128)S(1)} %copy-done.4, f32[34,18,258]{2,1,0:T(8,128)S(1)} %get-tuple-element.9, f32[32,16,256]{2,1,0:T(8,128)S(1)} %copy-done.10, f32[34,18,258]{2,1,0:T(8,128)S(1)} %get-tuple-element.8, f32[32,16,256]{2,1,0:T(8,128)S(1)} %copy-done.2, s32[32,16,256]{2,1,0:T(8,128)S(1)} %copy-done.9), kind=kLoop, calls=%fused_computation.90 | loop fusion | flops 7733248 | bytes 9961472 | tf_op jit(solution)/shard_map/add | solution.py:64
  39.8 4.3 %collective-permute-start.6 = (f32[32,1,256]{2,1,0:T(1,128)S(1)}, f32[32,1,256]{2,1,0:T(1,128)S(1)}, u32[]{:S(2)}, u32[]{:S(2)}) collective-permute-start(f32[32,1,256]{2,1,0:T(1,128)S(1)} %get-tuple-element.18), channel_id=1, source_target_pairs={{0,8},{8,16},{16,24},{1,9},{9,17},{17,25},{2,10},{10,18},{18,26},{... | collective-permute-start | bytes 98312 | tf_op jit(solution)/shard_map/ppermute | solution.py:16
  45.7 4.2 %collective-permute-done.7 = f32[32,1,256]{2,1,0:T(1,128)S(1)} collective-permute-done((f32[32,1,256]{2,1,0:T(1,128)S(1)}, f32[32,1,256]{2,1,0:T(1,128)S(1)}, u32[]{:S(2)}, u32[]{:S(2)}) %collective-permute-start.7) | collective-permute-done | bytes 32800 | tf_op jit(solution)/shard_map/ppermute | solution.py:19
  52.3 5.3 %collective-permute-start.8 = (f32[32,18,1]{2,1,0:T(8,128)}, f32[32,18,1]{2,1,0:T(8,128)}, u32[]{:S(2)}, u32[]{:S(2)}) collective-permute-start(f32[32,18,1]{2,1,0:T(8,128)} %get-tuple-element.17), channel_id=1, source_target_pairs={{0,2},{2,4},{4,6},{1,3},{3,5},{5,7},{8,10},{10,12},{12,14},{9,11},... | collective-permute-start | bytes 6920 | tf_op jit(solution)/shard_map/ppermute | solution.py:16
  57.8 5.1 %collective-permute-done.9 = f32[32,18,1]{2,1,0:T(8,128)} collective-permute-done((f32[32,18,1]{2,1,0:T(8,128)}, f32[32,18,1]{2,1,0:T(8,128)}, u32[]{:S(2)}, u32[]{:S(2)}) %collective-permute-start.9) | collective-permute-done | bytes 2336 | tf_op jit(solution)/shard_map/ppermute | solution.py:19
  64.1 1.5 pad_maximum_fusion.33
  66.9 3.2 %collective-permute-start.11 = (f32[1,18,258]{2,1,0:T(8,128)S(1)}, f32[1,18,258]{2,1,0:T(8,128)S(1)}, u32[]{:S(2)}, u32[]{:S(2)}) collective-permute-start(f32[1,18,258]{2,1,0:T(8,128)S(1)} %get-tuple-element.13), channel_id=1, source_target_pairs={{0,1},{2,3},{4,5},{6,7},{8,9},{10,11},{12,13},{14,15},{16,17},{18,... | collective-permute-start | bytes 55736 | tf_op jit(solution)/shard_map/ppermute | solution.py:16
  70.2 3.0 %multiply_add_fusion = f32[32,16,256]{2,1,0:T(8,128)} fusion(f32[32,16,256]{2,1,0:T(8,128)} %param.6, f32[34,18,258]{2,1,0:T(8,128)S(1)} %get-tuple-element.8, f32[32,16,256]{2,1,0:T(8,128)} %param.8, s32[32,16,256]{2,1,0:T(8,128)} %param.9), kind=kLoop, calls=%fused_computation.87 | loop fusion | flops 3538944 | bytes 5767168 | tf_op jit(solution)/shard_map/add | solution.py:63
  73.2 19.5 %reshape.45 = f32[8,4,4,4,64,4]{5,4,3,2,1,0:T(8,128)} reshape(f32[32,16,256]{2,1,0:T(8,128)} %multiply_add_fusion) | data formatting | bytes 1048576 | tf_op jit(solution)/shard_map/reshape | solution.py:76
  92.7 7.1 %reduce_sum.19 = f32[8,4,64]{2,1,0:T(4,128)S(1)} reduce(f32[8,4,4,4,64,4]{5,4,3,2,1,0:T(8,128)} %reshape.45, f32[]{:T(128)} %constant.7.clone.1), dimensions={1,3,5}, to_apply=%region_1.2 | reduce | flops 129024 | bytes 532484 | tf_op jit(solution)/shard_map/reduce_sum | solution.py:76
  99.7 6.9 %fusion.11 = f32[32,16,256]{2,1,0:T(8,128)} fusion(f32[32,16,256]{2,1,0:T(8,128)} %copy-done.5, f32[32,18,1]{2,1,0:T(8,128)} %collective-permute-done.8, f32[32,1,256]{2,1,0:T(1,128)S(1)} %collective-permute-done.7, f32[32,1,256]{2,1,0:T(1,128)S(1)} %collective-permute-done.6, f32[32,18,1]{2,1,0:T(8,128)} %collective-permute-done.9, ...), kind=kLoop, calls=%fused_computation.19 | loop fusion | flops 8650752 | bytes 6398752 | tf_op jit(solution)/shard_map/sub | solution.py:67
  106.7 19.5 %reshape.42 = f32[8,4,4,4,64,4]{5,4,3,2,1,0:T(8,128)} reshape(f32[32,16,256]{2,1,0:T(8,128)} %fusion.11) | data formatting | bytes 1048576 | tf_op jit(solution)/shard_map/reshape | solution.py:73
  126.1 7.1 %reduce_sum.18 = f32[8,4,64]{2,1,0:T(4,128)S(1)} reduce(f32[8,4,4,4,64,4]{5,4,3,2,1,0:T(8,128)} %reshape.42, f32[]{:T(128)} %constant.7.clone.1), dimensions={1,3,5}, to_apply=%region_0.1 | reduce | flops 129024 | bytes 532484 | tf_op jit(solution)/shard_map/reduce_sum | solution.py:73
  133.2 8.4 %all_gather.3 = f32[16,8,1,64]{3,1,2,0:T(8,128)S(1)} all-gather(f32[4,8,1,64]{3,1,2,0:T(8,128)S(1)} %copy.26), channel_id=1, replica_groups=mesh['gx'=4,'gy'=4,'gz'=2] {'gx'}, dimensions={0}, use_global_device_ids=true | all-gather | bytes 40960 | tf_op jit(solution)/shard_map/all_gather | solution.py:80
  142.4 1.8 %fusion = f32[8,4,1,64,1]{3,2,4,1,0:T(1,128)S(1)} fusion(f32[8,4,2,64,1]{3,4,2,1,0:T(1,128)S(1)} %bitcast.44, f32[8,4,1,2,64,64]{5,4,3,2,1,0:T(8,128)S(1)} %copy-done), kind=kOutput, calls=%fused_computation.2 | convolution fusion | flops 3145728 | bytes 1073152 | tf_op jit(solution)/shard_map/zxjkab,zxjkb->zxja/dot_general | solution.py:53
  144.2 7.9 %broadcast_in_dim.28 = f32[8,4,4,4,64,4]{5,4,3,2,1,0:T(8,128)} broadcast(f32[8,4,64]{2,1,0:T(4,128)S(1)} %multiply_divide_fusion), dimensions={0,2,4} | broadcast | bytes 532480 | tf_op jit(solution)/shard_map/broadcast_in_dim | solution.py:85
  152.2 15.1 %broadcast_in_dim.29 = f32[32,16,256]{2,1,0:T(8,128)S(1)} reshape(f32[8,4,4,4,64,4]{5,4,3,2,1,0:T(8,128)} %broadcast_in_dim.28) | data formatting | bytes 1048576 | tf_op jit(solution)/shard_map/broadcast_in_dim | solution.py:85
  (54 shorter events, 14.1 us)
Async XLA Ops:
  0.6 141.8 %copy-start = (f32[8,4,1,2,64,64]{5,4,3,2,1,0:T(8,128)S(1)}, f32[8,4,1,2,64,64]{5,4,3,2,1,0:T(8,128)}, u32[]{:S(2)}) copy-start(f32[8,4,1,2,64,64]{5,4,3,2,1,0:T(8,128)} %param.11) | copy-start | bytes 3145732
  2.1 6.7 %collective-permute-start = (f32[2,32,1,256]{3,2,1,0:T(1,128)S(1)}, f32[2,32,1,256]{3,2,1,0:T(1,128)S(1)}, u32[]{:S(2)}, u32[]{:S(2)}) collective-permute-start(f32[2,32,1,256]{3,2,1,0:T(1,128)S(1)} %get-tuple-element.14), channel_id=1, source_target_pairs={{0,8},{8,16},{16,24},{1,9},{9,17},{17,25},{2,10},{10,18},{18,26},{... | collective-permute-start | bytes 196616 | tf_op jit(solution)/shard_map/ppermute | solution.py:16
  6.9 6.2 %collective-permute-start.1 = (f32[2,32,1,256]{3,2,1,0:T(1,128)S(1)}, f32[2,32,1,256]{3,2,1,0:T(1,128)S(1)}, u32[]{:S(2)}, u32[]{:S(2)}) collective-permute-start(f32[2,32,1,256]{3,2,1,0:T(1,128)S(1)} %get-tuple-element.15), channel_id=1, source_target_pairs={{8,0},{16,8},{24,16},{9,1},{17,9},{25,17},{10,2},{18,10},{26,18},{... | collective-permute-start | bytes 196616 | tf_op jit(solution)/shard_map/ppermute | solution.py:19
  15.9 13.4 %copy-start.1 = (f32[32,16,256]{2,1,0:T(8,128)S(1)}, f32[32,16,256]{2,1,0:T(8,128)}, u32[]{:S(2)}) copy-start(f32[32,16,256]{2,1,0:T(8,128)} %param.8) | copy-start | bytes 1572868
  15.9 13.4 %copy-start.3 = (f32[32,16,256]{2,1,0:T(8,128)S(1)}, f32[32,16,256]{2,1,0:T(8,128)}, u32[]{:S(2)}) copy-start(f32[32,16,256]{2,1,0:T(8,128)} %param.6) | copy-start | bytes 1572868
  17.4 6.3 %collective-permute-start.2 = (f32[2,32,18,1]{1,0,3,2:T(2,128)S(1)}, f32[2,32,18,1]{1,0,3,2:T(2,128)S(1)}, u32[]{:S(2)}, u32[]{:S(2)}) collective-permute-start(f32[2,32,18,1]{1,0,3,2:T(2,128)S(1)} %copy.22), channel_id=1, source_target_pairs={{0,2},{2,4},{4,6},{1,3},{3,5},{5,7},{8,10},{10,12},{12,14},{9,11},... | collective-permute-start | bytes 13832 | tf_op jit(solution)/shard_map/ppermute | solution.py:16
  22.3 10.7 %copy-start.12 = (s32[8,4,1,2]{0,3,2,1:T(2,128)S(1)}, s32[8,4,1,2]{0,3,2,1:T(2,128)}, u32[]{:S(2)}) copy-start(s32[8,4,1,2]{0,3,2,1:T(2,128)} %param.10) | copy-start | bytes 772
  22.3 5.8 %collective-permute-start.3 = (f32[2,32,18,1]{1,0,3,2:T(2,128)S(1)}, f32[2,32,18,1]{1,0,3,2:T(2,128)S(1)}, u32[]{:S(2)}, u32[]{:S(2)}) collective-permute-start(f32[2,32,18,1]{1,0,3,2:T(2,128)S(1)} %copy.23), channel_id=1, source_target_pairs={{2,0},{4,2},{6,4},{3,1},{5,3},{7,5},{10,8},{12,10},{14,12},{11,9},... | collective-permute-start | bytes 13832 | tf_op jit(solution)/shard_map/ppermute | solution.py:19
  29.4 5.5 %copy-start.7 = (f32[2,32,18,1]{3,2,1,0:T(8,128)S(1)}, f32[2,32,18,1]{3,2,1,0:T(8,128)}, u32[]{:S(2)}) copy-start(f32[2,32,18,1]{3,2,1,0:T(8,128)} %copy.24) | copy-start | bytes 13828
  29.4 5.5 %copy-start.8 = (f32[2,32,18,1]{3,2,1,0:T(8,128)S(1)}, f32[2,32,18,1]{3,2,1,0:T(8,128)}, u32[]{:S(2)}) copy-start(f32[2,32,18,1]{3,2,1,0:T(8,128)} %copy.25) | copy-start | bytes 13828
  30.4 2.6 %collective-permute-start.4 = (f32[2,1,18,258]{3,2,1,0:T(8,128)S(1)}, f32[2,1,18,258]{3,2,1,0:T(8,128)S(1)}, u32[]{:S(2)}, u32[]{:S(2)}) collective-permute-start(f32[2,1,18,258]{3,2,1,0:T(8,128)S(1)} %get-tuple-element.6), channel_id=1, source_target_pairs={{0,1},{2,3},{4,5},{6,7},{8,9},{10,11},{12,13},{14,15},{16,17},{18,... | collective-permute-start | bytes 111464 | tf_op jit(solution)/shard_map/ppermute | solution.py:16
  31.7 3.2 %collective-permute-start.5 = (f32[2,1,18,258]{3,2,1,0:T(8,128)S(1)}, f32[2,1,18,258]{3,2,1,0:T(8,128)S(1)}, u32[]{:S(2)}, u32[]{:S(2)}) collective-permute-start(f32[2,1,18,258]{3,2,1,0:T(8,128)S(1)} %get-tuple-element.7), channel_id=1, source_target_pairs={{1,0},{3,2},{5,4},{7,6},{9,8},{11,10},{13,12},{15,14},{17,16},{19,... | collective-permute-start | bytes 111464 | tf_op jit(solution)/shard_map/ppermute | solution.py:19
  36.3 1.0 copy-start.2
  36.3 1.2 copy-start.4
  36.3 1.3 copy-start.9
  36.3 1.5 copy-start.10
  39.7 10.2 %copy-start.5 = (f32[32,16,256]{2,1,0:T(8,128)}, f32[32,16,256]{2,1,0:T(8,128)S(1)}, u32[]{:S(2)}) copy-start(f32[32,16,256]{2,1,0:T(8,128)S(1)} %fusion.48) | copy-start | bytes 1572868
  39.8 5.9 %collective-permute-start.6 = (f32[32,1,256]{2,1,0:T(1,128)S(1)}, f32[32,1,256]{2,1,0:T(1,128)S(1)}, u32[]{:S(2)}, u32[]{:S(2)}) collective-permute-start(f32[32,1,256]{2,1,0:T(1,128)S(1)} %get-tuple-element.18), channel_id=1, source_target_pairs={{0,8},{8,16},{16,24},{1,9},{9,17},{17,25},{2,10},{10,18},{18,26},{... | collective-permute-start | bytes 98312 | tf_op jit(solution)/shard_map/ppermute | solution.py:16
  44.1 5.8 %collective-permute-start.7 = (f32[32,1,256]{2,1,0:T(1,128)S(1)}, f32[32,1,256]{2,1,0:T(1,128)S(1)}, u32[]{:S(2)}, u32[]{:S(2)}) collective-permute-start(f32[32,1,256]{2,1,0:T(1,128)S(1)} %get-tuple-element.19), channel_id=1, source_target_pairs={{8,0},{16,8},{24,16},{9,1},{17,9},{25,17},{10,2},{18,10},{26,18},{... | collective-permute-start | bytes 98312 | tf_op jit(solution)/shard_map/ppermute | solution.py:19
  51.0 11.9 %collective-permute-start.9 = (f32[32,18,1]{2,1,0:T(8,128)}, f32[32,18,1]{2,1,0:T(8,128)}, u32[]{:S(2)}, u32[]{:S(2)}) collective-permute-start(f32[32,18,1]{2,1,0:T(8,128)} %get-tuple-element.16), channel_id=1, source_target_pairs={{2,0},{4,2},{6,4},{3,1},{5,3},{7,5},{10,8},{12,10},{14,12},{11,9},... | collective-permute-start | bytes 6920 | tf_op jit(solution)/shard_map/ppermute | solution.py:19
  52.3 11.8 %collective-permute-start.8 = (f32[32,18,1]{2,1,0:T(8,128)}, f32[32,18,1]{2,1,0:T(8,128)}, u32[]{:S(2)}, u32[]{:S(2)}) collective-permute-start(f32[32,18,1]{2,1,0:T(8,128)} %get-tuple-element.17), channel_id=1, source_target_pairs={{0,2},{2,4},{4,6},{1,3},{3,5},{5,7},{8,10},{10,12},{12,14},{9,11},... | collective-permute-start | bytes 6920 | tf_op jit(solution)/shard_map/ppermute | solution.py:16
  65.7 34.1 %collective-permute-start.10 = (f32[1,18,258]{2,1,0:T(8,128)}, f32[1,18,258]{2,1,0:T(8,128)S(1)}, u32[]{:S(2)}, u32[]{:S(2)}) collective-permute-start(f32[1,18,258]{2,1,0:T(8,128)} %get-tuple-element.12), channel_id=1, source_target_pairs={{1,0},{3,2},{5,4},{7,6},{9,8},{11,10},{13,12},{15,14},{17,16},{19,... | collective-permute-start | bytes 55736 | tf_op jit(solution)/shard_map/ppermute | solution.py:19
  66.9 32.8 %collective-permute-start.11 = (f32[1,18,258]{2,1,0:T(8,128)S(1)}, f32[1,18,258]{2,1,0:T(8,128)S(1)}, u32[]{:S(2)}, u32[]{:S(2)}) collective-permute-start(f32[1,18,258]{2,1,0:T(8,128)S(1)} %get-tuple-element.13), channel_id=1, source_target_pairs={{0,1},{2,3},{4,5},{6,7},{8,9},{10,11},{12,13},{14,15},{16,17},{18,... | collective-permute-start | bytes 55736 | tf_op jit(solution)/shard_map/ppermute | solution.py:16
  144.2 7.9 %copy-start.11 = (f32[8,4,64]{2,1,0:T(4,128)}, f32[8,4,64]{2,1,0:T(4,128)S(1)}, u32[]{:S(2)}) copy-start(f32[8,4,64]{2,1,0:T(4,128)S(1)} %multiply_divide_fusion) | copy-start | bytes 24580
  152.2 15.1 %copy-start.6 = (f32[32,16,256]{2,1,0:T(8,128)S(1)}, f32[32,16,256]{2,1,0:T(8,128)}, u32[]{:S(2)}) copy-start(f32[32,16,256]{2,1,0:T(8,128)} %copy-done.5) | copy-start | bytes 1572868
where the time goes:
time: 169 us; the launch traced here: 168 us
  local copies, waits for them, and re-layouts  72.4 us (43%)
  other arithmetic  33.8 us (20%)
  starting transfers between devices  30.3 us (18%)
  waiting for transfers between devices  20.5 us (12%)
  blocking collectives  8.44 us (5%)
  matrix products  1.76 us (1%)
    broadcast_in_dim x2, local copies, waits for them, and re-layouts, per_device(): jnp.broadcast_to(correction[:, None, :, None, :, :, None], (coarse_z, 4,...  23 us
    ppermute x6, starting transfers between devices, padded_2(): lax.ppermute(lax.slice_in_dim(block, block.shape[dim] - width, None, axis...  22.4 us
    reshape x1, local copies, waits for them, and re-layouts, per_device(): residual.reshape(coarse_z, 4, coarse_x, 4, y_aggs, agg_size, 4)  19.5 us
    reshape x1, local copies, waits for them, and re-layouts, per_device(): diagonal.reshape(coarse_z, 4, coarse_x, 4, y_aggs, agg_size, 4)  19.5 us
    ppermute x6, waiting for transfers between devices, padded_2(): lax.ppermute(lax.slice_in_dim(block, 0, width, axis=dim), axis, backward)  18.5 us
    all_gather x1, blocking collectives, per_device(): gathered = lax.all_gather(resid_xfirst, 'gx', axis=0, tiled=True)  8.44 us
    ppermute x6, starting transfers between devices, padded_2(): lax.ppermute(lax.slice_in_dim(block, 0, width, axis=dim), axis, backward)  7.85 us
    reduce_sum x1, other arithmetic, per_device(): diagonal.reshape(coarse_z, 4, coarse_x, 4, y_aggs, agg_size, 4)  7.05 us
  transfers between devices with their start and end apart: 12, of which 8 were waited for; matrix products, arithmetic and copies ran while one was open for 19% of the time, Pallas kernels for 0%

commit v1 on v0

v1 whole, which is shorter than its diff:
```python
import functools

import jax
import jax.numpy as jnp
from jax import lax
from jax.experimental import pallas as pl
from jax.experimental.pallas import tpu as pltpu
from jax.sharding import PartitionSpec as P

OMEGA = 0.8
CHARGE_SCALE = 40.0
COARSE_SCALE = 4.0
MESH = pl.DeviceIdType.MESH
F32 = jnp.float32
BF16 = jnp.bfloat16


def split2(value):
    high = value.astype(BF16)
    return high, (value - high.astype(F32)).astype(BF16)


def kernel(counts, Z, X, Y, A, pat, pot_h, chg_h, eps_h, lab_h, blk_h, out, corr,
           pot, chg, eps, lab, blk, num, dia, scr, wxs, wys, swp,
           zlo, zhi, xlo, xhi, ylo, yhi, xs_lo, xs_hi, ys,
           zlo2, zhi2, xlo2, xhi2, ylo2, yhi2, xs_lo2, xs_hi2, ys2,
           fx, zsr, zsd, weights, mine, col, picks, spread,
           in_sem, send_sem, recv_sem, gsend, grecv):
    ids = [lax.axis_index(name) for name in ("gx", "gy", "gz")]
    CZ, CX = Z // 4, X // 4
    NC = CZ * CX
    half = Y // 2

    loads = [pltpu.make_async_copy(s, d, in_sem.at[i])
             for i, (s, d) in enumerate(((pot_h, pot), (eps_h, eps), (chg_h, chg), (lab_h, lab), (blk_h, blk)))]
    for load in loads:
        load.start()

    def at(axis, index):
        return tuple(index if a == axis else ids[a] for a in range(3))

    def low_ok(axis):
        return ids[axis] > 0

    def high_ok(axis):
        return ids[axis] < counts[axis] - 1

    barrier = pltpu.get_barrier_semaphore()
    n = counts[0]
    for d in range(1, n):
        pl.semaphore_signal(barrier, inc=1, device_id=at(0, lax.rem(ids[0] + d, n)), device_id_type=MESH)
    expected = n - 1
    for axis in (1, 2):
        for ok, step in ((low_ok(axis), -1), (high_ok(axis), 1)):
            target = jnp.clip(ids[axis] + step, 0, counts[axis] - 1)

            @pl.when(ok)
            def _(target=target, axis=axis):
                pl.semaphore_signal(barrier, inc=1, device_id=at(axis, target), device_id_type=MESH)
            expected = expected + ok.astype(jnp.int32)

    for axis, lo_bufs, hi_bufs in ((2, (zlo, zlo2), (zhi, zhi2)), (0, (xlo, xlo2), (xhi, xhi2)), (1, (ylo, ylo2), (yhi, yhi2))):
        @pl.when(jnp.logical_not(low_ok(axis)))
        def _(bufs=lo_bufs):
            for b in bufs:
                b[...] = jnp.zeros_like(b)

        @pl.when(jnp.logical_not(high_ok(axis)))
        def _(bufs=hi_bufs):
            for b in bufs:
                b[...] = jnp.zeros_like(b)

    def up(axis, src, dst, sem):
        return (axis, True, pltpu.make_async_remote_copy(
            src_ref=src, dst_ref=dst, send_sem=send_sem.at[sem], recv_sem=recv_sem.at[sem],
            device_id=at(axis, jnp.minimum(ids[axis] + 1, counts[axis] - 1)), device_id_type=MESH))

    def down(axis, src, dst, sem):
        return (axis, False, pltpu.make_async_remote_copy(
            src_ref=src, dst_ref=dst, send_sem=send_sem.at[sem], recv_sem=recv_sem.at[sem],
            device_id=at(axis, jnp.maximum(ids[axis] - 1, 0)), device_id_type=MESH))

    def start(messages):
        for axis, upward, copy in messages:
            @pl.when(high_ok(axis) if upward else low_ok(axis))
            def _(copy=copy):
                copy.start()

    def wait_recv(messages):
        for axis, upward, copy in messages:
            @pl.when(low_ok(axis) if upward else high_ok(axis))
            def _(copy=copy):
                copy.wait_recv()

    def wait_send(messages):
        for axis, upward, copy in messages:
            @pl.when(high_ok(axis) if upward else low_ok(axis))
            def _(copy=copy):
                copy.wait_send()

    def slab(z):
        return pl.ds(pl.multiple_of(z * X, X), X)

    lane = lax.broadcasted_iota(jnp.int32, (X, 128), 1)
    pair = lane // 2
    row = lax.broadcasted_iota(jnp.int32, (X, Y), 0)
    ylane = lax.broadcasted_iota(jnp.int32, (X, Y), 1)

    def ends(value):
        return jnp.where(lane == 127, value[:, half:][:, -128:], value[:, :128])

    loads[0].wait()
    loads[1].wait()
    def pack1(z, acc):
        acc = jnp.where(pair == z, pltpu.roll(ends(pot[slab(z), :]), 2 * z + 1, 1), acc)
        return jnp.where(pair == z + 32, pltpu.roll(ends(eps[slab(z), :]), 2 * z + 65, 1), acc)
    ys[...] = lax.fori_loop(0, Z, pack1, jnp.zeros((X, 128), F32), unroll=8)
    for z in range(Z):
        for k, field in enumerate((pot, eps)):
            xs_lo[k * Z + z:k * Z + z + 1, :] = field[z * X:z * X + 1, :]
            xs_hi[k * Z + z:k * Z + z + 1, :] = field[z * X + X - 1:z * X + X, :]
    pl.semaphore_wait(barrier, expected)
    first = pl.ds(0, X)
    last = pl.ds((Z - 1) * X, X)
    halo1 = [
        up(0, xs_hi, xlo, 0), down(0, xs_lo, xhi, 1),
        up(1, ys, ylo, 2), down(1, ys, yhi, 3),
        up(2, pot.at[last, :], zlo.at[pl.ds(0, X), :], 4), up(2, eps.at[last, :], zlo.at[pl.ds(X, X), :], 5),
        down(2, pot.at[first, :], zhi.at[pl.ds(0, X), :], 6), down(2, eps.at[first, :], zhi.at[pl.ds(X, X), :], 7),
    ]
    start(halo1)
    loads[2].wait()
    loads[3].wait()

    not_top = row < X - 1
    not_end = ylane < Y - 1

    def sweep_local(z, carry):
        fz_prev, wz_prev = carry
        v, e = pot[slab(z), :], eps[slab(z), :]
        up_z = jnp.minimum(z + 1, Z - 1)
        inside = jnp.where(z < Z - 1, 0.5, 0.0).astype(F32)
        wz = inside * (e + eps[slab(up_z), :])
        fz = wz * (v - pot[slab(up_z), :])
        wx = jnp.where(not_top, 0.5 * (e + pltpu.roll(e, X - 1, 0)), 0.0)
        fxl = wx * (v - pltpu.roll(v, X - 1, 0))
        wy = jnp.where(not_end, 0.5 * (e + pltpu.roll(e, Y - 1, 1)), 0.0)
        fyl = wy * (v - pltpu.roll(v, Y - 1, 1))
        flux = (fz - fz_prev) + (fxl - pltpu.roll(fxl, 1, 0)) + (fyl - pltpu.roll(fyl, 1, 1))
        faces = (wz + wz_prev) + (wx + pltpu.roll(wx, 1, 0)) + (wy + pltpu.roll(wy, 1, 1))
        labels = lab[slab(z), :]
        s = e * jnp.where(labels == 1, 0.05, jnp.where(labels == 2, 0.2, 0.0))
        ep, em = jnp.exp(v), jnp.exp(-v)
        wxs[slab(z), :] = wx
        wys[slab(z), :] = wy
        scr[slab(z), :] = s
        num[slab(z), :] = CHARGE_SCALE * chg[slab(z), :] - flux - s * (0.5 * (ep - em))
        dia[slab(z), :] = faces + s * (0.5 * (ep + em))
        return fz, wz
    zero = jnp.zeros((X, Y), F32)
    lax.fori_loop(0, Z, sweep_local, (zero, zero), unroll=2)

    wait_recv(halo1)
    wz_lo = 0.5 * (eps[first, :] + zlo[X:2 * X, :])
    wz_hi = 0.5 * (eps[last, :] + zhi[X:2 * X, :])
    num[first, :] = num[first, :] - wz_lo * (pot[first, :] - zlo[0:X, :])
    num[last, :] = num[last, :] - wz_hi * (pot[last, :] - zhi[0:X, :])
    dia[first, :] = dia[first, :] + wz_lo
    dia[last, :] = dia[last, :] + wz_hi
    for k, (own, halo) in enumerate(((xs_lo, xlo), (xs_hi, xhi))):
        w = 0.5 * (own[Z:2 * Z, :] + halo[Z:2 * Z, :])
        fx[2 * k * Z:(2 * k + 1) * Z, :] = w * (own[0:Z, :] - halo[0:Z, :])
        fx[(2 * k + 1) * Z:(2 * k + 2) * Z, :] = w
    even = lane % 2 == 0
    own_y = pltpu.roll(ys[...], 127, 1)
    halo_y = jnp.where(even, ylo[...], pltpu.roll(yhi[...], 126, 1))
    wy_end = 0.5 * (pltpu.roll(own_y, 64, 1) + pltpu.roll(halo_y, 64, 1))
    fy_end = wy_end * (own_y - halo_y)

    def at_ends(value):
        return jnp.concatenate([jnp.where(lane == 0, value, 0.0), jnp.where(lane == 127, value, 0.0)], axis=1)

    def sweep(zc, acc):
        total = jnp.zeros((X, Y), F32)
        for dz in range(4):
            z = zc * 4 + dz
            shift = lax.rem(128 - 2 * z, 128)
            f = at_ends(pltpu.roll(fy_end, shift, 1))
            w = at_ends(pltpu.roll(wy_end, shift, 1))
            f = f + jnp.where(row == 0, fx[pl.ds(z, 1), :], 0.0) + jnp.where(row == X - 1, fx[pl.ds(2 * Z + z, 1), :], 0.0)
            w = w + jnp.where(row == 0, fx[pl.ds(Z + z, 1), :], 0.0) + jnp.where(row == X - 1, fx[pl.ds(3 * Z + z, 1), :], 0.0)
            d = dia[slab(z), :] + w
            total = total + d
            sw = pot[slab(z), :] + OMEGA * (num[slab(z), :] - f) / d
            swp[slab(z), :] = sw
            xs_lo2[pl.ds(z, 1), :] = sw[0:1, :]
            xs_hi2[pl.ds(z, 1), :] = sw[X - 1:X, :]
            acc = jnp.where(pair == z, pltpu.roll(ends(sw), 2 * z + 1, 1), acc)
        zsd[slab(zc), :] = total
        return acc
    ys2[...] = lax.fori_loop(0, CZ, sweep, jnp.zeros((X, 128), F32))

    halo2 = [
        up(0, xs_hi2, xlo2, 8), down(0, xs_lo2, xhi2, 9),
        up(1, ys2, ylo2, 10), down(1, ys2, yhi2, 11),
        up(2, swp.at[last, :], zlo2, 12), down(2, swp.at[first, :], zhi2, 13),
    ]
    start(halo2)

    def residual_local(zc, fz_prev):
        total = jnp.zeros((X, Y), F32)
        for dz in range(4):
            z = zc * 4 + dz
            v, e = swp[slab(z), :], eps[slab(z), :]
            up_z = jnp.minimum(z + 1, Z - 1)
            inside = jnp.where(z < Z - 1, 0.5, 0.0).astype(F32)
            fz = inside * (e + eps[slab(up_z), :]) * (v - swp[slab(up_z), :])
            fxl = wxs[slab(z), :] * (v - pltpu.roll(v, X - 1, 0))
            fyl = wys[slab(z), :] * (v - pltpu.roll(v, Y - 1, 1))
            flux = (fz - fz_prev) + (fxl - pltpu.roll(fxl, 1, 0)) + (fyl - pltpu.roll(fyl, 1, 1))
            total = total + (CHARGE_SCALE * chg[slab(z), :] - flux - scr[slab(z), :] * (0.5 * (jnp.exp(v) - jnp.exp(-v))))
            fz_prev = fz
        zsr[slab(zc), :] = total
        return fz_prev
    lax.fori_loop(0, CZ, residual_local, zero)

    loads[4].wait()
    def split_blocks(zc, c):
        for xc in range(CX):
            at_block = (zc * CX + xc) * 2
            both = jnp.concatenate([blk[at_block], blk[at_block + 1]], axis=1)
            high, low = split2(both)
            weights[zc, xc * A:(xc + 1) * A, 0:2 * A] = high
            weights[zc, xc * A:(xc + 1) * A, 2 * A:4 * A] = low
        return c
    lax.fori_loop(0, CZ, split_blocks, 0)

    merge = jnp.where(lax.broadcasted_iota(jnp.int32, (Y, 128), 0) // 4 == lax.broadcasted_iota(jnp.int32, (Y, 128), 1) % A, 1.0, 0.0).astype(BF16)

    def coarse_rows(ref):
        groups = []
        for xc in range(CX):
            rows = []
            for zc in range(CZ):
                base = zc * X + 4 * xc
                block = ref[zc * X + (xc // 2) * 8:zc * X + (xc // 2) * 8 + 8, :]
                rows.append(jnp.sum(block[(xc % 2) * 4:(xc % 2) * 4 + 4, :], axis=0, keepdims=True))
            groups.append(jnp.concatenate(rows, axis=0))
        return groups

    def merged(groups):
        high, low = split2(jnp.concatenate(groups, axis=0))
        both = jnp.dot(jnp.concatenate([high, low], axis=0), merge, preferred_element_type=F32)
        return (both[0:NC, :] + both[NC:2 * NC, :]) * (1.0 / 64.0)

    coarse_diag = merged(coarse_rows(zsd))

    wait_recv(halo2)
    zsr[0:X, :] = zsr[0:X, :] - wz_lo * (swp[first, :] - zlo2[...])
    zsr[(CZ - 1) * X:CZ * X, :] = zsr[(CZ - 1) * X:CZ * X, :] - wz_hi * (swp[last, :] - zhi2[...])
    own_y = pltpu.roll(ys2[...], 127, 1)
    halo_y = jnp.where(even, ylo2[...], pltpu.roll(yhi2[...], 126, 1))
    f = wy_end * (own_y - halo_y)
    f = f + pltpu.roll(f, 126, 1)
    f = f + pltpu.roll(f, 124, 1)
    for zc in range(CZ):
        zsr[zc * X:(zc + 1) * X, :] = zsr[zc * X:(zc + 1) * X, :] - at_ends(pltpu.roll(f, (128 - 8 * zc) % 128, 1))
    groups = coarse_rows(zsr)
    for k, (own, halo, xc) in enumerate(((xs_lo2, xlo2, 0), (xs_hi2, xhi2, CX - 1))):
        f = fx[(2 * k + 1) * Z:(2 * k + 2) * Z, :] * (own[...] - halo[...])
        groups[xc] = groups[xc] - jnp.concatenate(
            [jnp.sum(f[4 * zc:4 * zc + 4, :], axis=0, keepdims=True) for zc in range(CZ)], axis=0)
    coarse_resid = merged(groups)
    mine[...] = coarse_resid
    my_rows = pl.ds(pl.multiple_of(ids[0] * NC, NC), NC)
    gathers = []
    for d in range(1, n):
        copy = pltpu.make_async_remote_copy(
            src_ref=mine, dst_ref=col.at[my_rows, :], send_sem=gsend.at[d - 1], recv_sem=grecv.at[d - 1],
            device_id=at(0, lax.rem(ids[0] + d, n)), device_id_type=MESH)
        copy.start()
        gathers.append(copy)
    col[my_rows, :] = coarse_resid
    for copy in gathers:
        copy.wait_recv()

    left = lax.broadcasted_iota(jnp.int32, (1, 128), 1) < A
    for zc in range(CZ):
        for xc in range(CX):
            p = jnp.where(left, col[pl.ds(pat[zc, xc, 0, 0], 1), :], col[pl.ds(pat[zc, xc, 0, 1], 1), :])
            picks[zc * 8 + xc:zc * 8 + xc + 1, :] = p
            picks[zc * 8 + 4 + xc:zc * 8 + 5 + xc, :] = p
    half_row = lax.broadcasted_iota(jnp.int32, (8, 128), 0) < 4
    own_block = (lax.broadcasted_iota(jnp.int32, (8, 4 * A), 0) % 4) == (lax.broadcasted_iota(jnp.int32, (8, 4 * A), 1) // A)
    rows = []
    for zc in range(CZ):
        p = picks[zc * 8:zc * 8 + 8, :]
        high = p.astype(BF16).astype(F32)
        lhs = jnp.concatenate([jnp.where(half_row, high, p - high), jnp.where(half_row, high, 0.0)], axis=1).astype(BF16)
        prod = lax.dot_general(lhs, weights[zc], (((1,), (1,)), ((), ())), preferred_element_type=F32)
        rows.append(jnp.sum(jnp.where(own_block, prod, 0.0), axis=0, keepdims=True))
    coupled = jnp.concatenate(rows, axis=0)

    def by_lane(value):
        parts = [value[xc * CZ:(xc + 1) * CZ, :] for xc in range(CX)]
        return jnp.concatenate([jnp.where(left, parts[i], parts[i + 1]) for i in range(0, CX, 2)], axis=1)

    correction = COARSE_SCALE * (by_lane(coarse_resid) + coupled) / by_lane(coarse_diag)
    for xc in range(CX):
        corr[:, xc, 0, :] = correction[:, xc * A:(xc + 1) * A]
    stacked = []
    for xc in range(CX):
        part = correction[:, (xc // 2) * 128:(xc // 2) * 128 + 128]
        stacked.append(jnp.where(left if xc % 2 == 0 else jnp.logical_not(left), part, 0.0))
    high, low = split2(jnp.concatenate(stacked, axis=0))
    both = lax.dot_general(jnp.concatenate([high, low], axis=0), merge, (((1,), (1,)), ((), ())), preferred_element_type=F32)
    spread[...] = both[0:NC, :] + both[NC:2 * NC, :]
    quarter = row // 4

    def finish(zc, c):
        add = jnp.zeros((X, Y), F32)
        for xc in range(CX):
            add = jnp.where(quarter == xc, spread[pl.ds(xc * CZ + zc, 1), :], add)
        for dz in range(4):
            z = zc * 4 + dz
            out[slab(z), :] = swp[slab(z), :] + add
        return c
    lax.fori_loop(0, CZ, finish, 0)

    wait_send(halo1)
    wait_send(halo2)
    for copy in gathers:
        copy.wait_send()


def solution(mesh):
    counts = (mesh.shape["gx"], mesh.shape["gy"], mesh.shape["gz"])

    def per_device(potential, charge, permittivity, labels, pattern, blocks):
        Z, X, Y = potential.shape
        A = blocks.shape[-1]
        CZ, CX = Z // 4, X // 4
        NC = CZ * CX
        flat = (Z * X, Y)
        whole = pltpu.VMEM(flat, F32)
        any_spec = pl.BlockSpec(memory_space=pl.ANY)
        vmem = pl.BlockSpec(memory_space=pltpu.VMEM)
        n = counts[0]

        def halo_scratch(k):
            return [pltpu.VMEM((k * X, Y), F32)] * 2 + [pltpu.VMEM((k * Z, Y), F32)] * 2 + [pltpu.VMEM((X, 128), F32)] * 2 + \
                [pltpu.VMEM((k * Z, Y), F32)] * 2 + [pltpu.VMEM((X, 128), F32)]

        out, corr = pl.pallas_call(
            functools.partial(kernel, counts, Z, X, Y, A),
            out_shape=(jax.ShapeDtypeStruct(flat, F32), jax.ShapeDtypeStruct((CZ, CX, 1, A), F32)),
            in_specs=[pl.BlockSpec(memory_space=pltpu.SMEM)] + [any_spec] * 5,
            out_specs=(vmem, vmem),
            scratch_shapes=[
                whole, whole, whole, pltpu.VMEM(flat, jnp.int32), pltpu.VMEM((2 * NC, A, A), F32),
                whole, whole, whole, whole, whole, whole,
                *halo_scratch(2), *halo_scratch(1),
                pltpu.VMEM((4 * Z, Y), F32), pltpu.VMEM((CZ * X, Y), F32), pltpu.VMEM((CZ * X, Y), F32),
                pltpu.VMEM((CZ, CX * A, 4 * A), BF16), pltpu.VMEM((NC, 128), F32), pltpu.VMEM((n * NC, 128), F32),
                pltpu.VMEM((8 * CZ, 128), F32), pltpu.VMEM((NC, Y), F32),
                pltpu.SemaphoreType.DMA((5,)), pltpu.SemaphoreType.DMA((14,)), pltpu.SemaphoreType.DMA((14,)),
                pltpu.SemaphoreType.DMA((n,)), pltpu.SemaphoreType.DMA((n,)),
            ],
            compiler_params=pltpu.CompilerParams(
                collective_id=0, has_side_effects=True, vmem_limit_bytes=32 * 1024 * 1024),
        )(pattern, potential.reshape(flat), charge.reshape(flat), permittivity.reshape(flat), labels.reshape(flat),
          blocks.reshape(2 * NC, A, A))
        return out.reshape(Z, X, Y), corr

    return jax.shard_map(
        per_device,
        mesh=mesh,
        in_specs=(
            P("gz", "gx", "gy"),
            P("gz", "gx", "gy"),
            P("gz", "gx", "gy"),
            P("gz", "gx", "gy"),
            P("gz", "gx", "gy", None),
            P("gz", "gx", "gy", None, None, None),
        ),
        out_specs=(P("gz", "gx", "gy"), P("gz", "gx", "gy", None)),
        check_vma=False,
    )
```

time: 169 us -> 27.5 us (0.16)
  local copies, waits for them, and re-layouts: 72.4 us -> 7.94 us
  other arithmetic: 33.8 us -> 0 us
  starting transfers between devices: 30.3 us -> 0 us
  waiting for transfers between devices: 20.5 us -> 0 us
  Pallas kernels: 0 us -> 18.5 us
  blocking collectives: 8.44 us -> 0 us
  matrix products: 1.76 us -> 0 us
    reshape x2 -> x0, local copies, waits for them, and re-layouts: 38.9 us -> none  [the longest x1 19.5 us: per_device(): residual.reshape(coarse_z, 4, coarse_x, 4, y_aggs, agg_size, 4)]
    ppermute x12 -> x0, starting transfers between devices: 30.3 us -> none  [the longest x6 22.4 us: padded_2(): lax.ppermute(lax.slice_in_dim(block, block.shape[dim] - width, None, axis...]
    broadcast_in_dim x2 -> x0, local copies, waits for them, and re-layouts: 23 us -> none  [per_device(): jnp.broadcast_to(correction[:, None, :, None, :, :, None], (coarse_z, 4,...]
    ppermute x12 -> x0, waiting for transfers between devices: 20.5 us -> none  [the longest x6 18.5 us: padded_2(): lax.ppermute(lax.slice_in_dim(block, 0, width, axis=dim), axis, backward)]
    pallas_call x0 -> x1, Pallas kernels: none -> 18.5 us  [per_device(): pl.pallas_call(functools.partial(kernel, counts, Z, X, Y, A), out_shape=(...]
    reduce_sum x2 -> x0, other arithmetic: 14.1 us -> none  [the longest x1 7.05 us: per_device(): diagonal.reshape(coarse_z, 4, coarse_x, 4, y_aggs, agg_size, 4)]
    all_gather x1 -> x0, blocking collectives: 8.44 us -> none  [per_device(): gathered = lax.all_gather(resid_xfirst, 'gx', axis=0, tiled=True)]
    sub x1 -> x0, other arithmetic: 6.91 us -> none  [per_device(): residual = source - swept_flux - screening * jnp.sinh(swept)]
  transfers between devices with their start and end apart: 12 -> 0, of which waited for: 8 -> 0; matrix products, arithmetic and copies ran while one was open for 19% -> 0% of each run, Pallas kernels for 0% -> 0%
where the time goes in v1:
time: 27.5 us; the launch traced here: 27.1 us
  Pallas kernels  18.5 us (67%)
  local copies, waits for them, and re-layouts  7.94 us (29%)
  between operations  0.64 us (2%)
    pallas_call x1, Pallas kernels, per_device(): pl.pallas_call(functools.partial(kernel, counts, Z, X, Y, A), out_shape=(...  18.5 us
    unnamed x13, local copies, waits for them, and re-layouts  7.94 us

profile of v1, /device:TPU:0, one launch (start us, length us, event | category | flops | bytes accessed | tf_op | source)
XLA Modules:
  0.0 27.1 jit_solution(1640436144701442547)
XLA Ops:
  0.6 0.8 %copy.8.pat = s32[8,4,1,2]{3,2,1,0:T(1,128)S(1)} copy(s32[8,4,1,2]{0,3,2,1:T(2,128)} %param.10) | data formatting | bytes 512 | tf_op args[4]
  1.4 0.0 copy-start
  1.4 1.6 %copy-done = f32[8,4,1,2,64,64]{5,4,3,2,1,0:T(8,128)S(1)} copy-done((f32[8,4,1,2,64,64]{5,4,3,2,1,0:T(8,128)S(1)}, f32[8,4,1,2,64,64]{5,4,3,2,1,0:T(8,128)}, u32[]{:S(2)}) %copy-start) | copy-done | bytes 1048600
  3.0 0.0 copy-start.1
  3.0 1.0 %copy-done.1 = f32[32,16,256]{2,1,0:T(8,128)S(1)} copy-done((f32[32,16,256]{2,1,0:T(8,128)S(1)}, f32[32,16,256]{2,1,0:T(8,128)}, u32[]{:S(2)}) %copy-start.1) | copy-done | bytes 524312
  4.0 0.0 copy-start.2
  4.1 1.0 %copy-done.2 = f32[32,16,256]{2,1,0:T(8,128)S(1)} copy-done((f32[32,16,256]{2,1,0:T(8,128)S(1)}, f32[32,16,256]{2,1,0:T(8,128)}, u32[]{:S(2)}) %copy-start.2) | copy-done | bytes 524312
  5.1 0.0 copy-start.3
  5.1 1.0 %copy-done.3 = f32[32,16,256]{2,1,0:T(8,128)S(1)} copy-done((f32[32,16,256]{2,1,0:T(8,128)S(1)}, f32[32,16,256]{2,1,0:T(8,128)}, u32[]{:S(2)}) %copy-start.3) | copy-done | bytes 524312
  6.1 0.0 copy-start.4
  6.1 1.0 %copy-done.4 = s32[32,16,256]{2,1,0:T(8,128)S(1)} copy-done((s32[32,16,256]{2,1,0:T(8,128)S(1)}, s32[32,16,256]{2,1,0:T(8,128)}, u32[]{:S(2)}) %copy-start.4) | copy-done | bytes 524312
  7.2 18.5 %shard_map.77 = (f32[512,256]{1,0:T(8,128)S(1)}, f32[8,4,1,64]{3,2,1,0:T(1,128)S(1)}) custom-call(s32[8,4,1,2]{3,2,1,0:T(1,128)S(1)} %copy.8.pat, f32[512,256]{1,0:T(8,128)S(1)} %bitcast.8, f32[512,256]{1,0:T(8,128)S(1)} %bitcast.9, f32[512,256]{1,0:T(8,128)S(1)} %bitcast.10, s32[512,256]{1,0:T(8,128)S(1)} %bitcast.11, f32[64,64,64]{2,1,0:T(8,128)S(1)} %bitcast.6), custom_call_target="tpu_custom_call" | custom-call | tf_op jit(solution)/shard_map/pallas_call | solution.py:354
  25.7 0.8 %copy.11 = f32[32,16,256]{2,1,0:T(8,128)} copy(f32[32,16,256]{2,1,0:T(8,128)S(1)} %bitcast.7) | data formatting | bytes 1048576
  26.5 0.6 %copy.12 = f32[8,4,1,64]{3,2,1,0:T(1,128)} copy(f32[8,4,1,64]{3,2,1,0:T(1,128)S(1)} %get-tuple-element.9) | data formatting | bytes 16384
Async XLA Ops:
  1.4 1.6 %copy-start = (f32[8,4,1,2,64,64]{5,4,3,2,1,0:T(8,128)S(1)}, f32[8,4,1,2,64,64]{5,4,3,2,1,0:T(8,128)}, u32[]{:S(2)}) copy-start(f32[8,4,1,2,64,64]{5,4,3,2,1,0:T(8,128)} %param.11) | copy-start | bytes 3145732
  3.0 1.0 %copy-start.1 = (f32[32,16,256]{2,1,0:T(8,128)S(1)}, f32[32,16,256]{2,1,0:T(8,128)}, u32[]{:S(2)}) copy-start(f32[32,16,256]{2,1,0:T(8,128)} %param.6) | copy-start | bytes 1572868
  4.0 1.0 %copy-start.2 = (f32[32,16,256]{2,1,0:T(8,128)S(1)}, f32[32,16,256]{2,1,0:T(8,128)}, u32[]{:S(2)}) copy-start(f32[32,16,256]{2,1,0:T(8,128)} %param.7) | copy-start | bytes 1572868
  5.1 1.0 %copy-start.3 = (f32[32,16,256]{2,1,0:T(8,128)S(1)}, f32[32,16,256]{2,1,0:T(8,128)}, u32[]{:S(2)}) copy-start(f32[32,16,256]{2,1,0:T(8,128)} %param.8) | copy-start | bytes 1572868
  6.1 1.0 %copy-start.4 = (s32[32,16,256]{2,1,0:T(8,128)S(1)}, s32[32,16,256]{2,1,0:T(8,128)}, u32[]{:S(2)}) copy-start(s32[32,16,256]{2,1,0:T(8,128)} %param.9) | copy-start | bytes 1572868

commit v2 on v1

--- a/solution.py
+++ b/solution.py
@@ -20,11 +20,11 @@
     return high, (value - high.astype(F32)).astype(BF16)
 
 
-def kernel(counts, Z, X, Y, A, pat, pot_h, chg_h, eps_h, lab_h, blk_h, out, corr,
-           pot, chg, eps, lab, blk, num, dia, scr, wxs, wys, swp,
+def kernel(counts, Z, X, Y, A, pat_h, pot_h, chg_h, eps_h, lab_h, blk_h, out, corr,
+           pat, pot, chg, eps, lab, blk, num, dia, scr, wxs, wys, swp,
            zlo, zhi, xlo, xhi, ylo, yhi, xs_lo, xs_hi, ys,
            zlo2, zhi2, xlo2, xhi2, ylo2, yhi2, xs_lo2, xs_hi2, ys2,
-           fx, zsr, zsd, weights, mine, col, picks, spread,
+           fx, zsr, zsd, weights, mine, col, choose, spread,
            in_sem, send_sem, recv_sem, gsend, grecv):
     ids = [lax.axis_index(name) for name in ("gx", "gy", "gz")]
     CZ, CX = Z // 4, X // 4
@@ -32,8 +32,8 @@
     half = Y // 2
 
     loads = [pltpu.make_async_copy(s, d, in_sem.at[i])
-             for i, (s, d) in enumerate(((pot_h, pot), (eps_h, eps), (chg_h, chg), (lab_h, lab), (blk_h, blk)))]
-    for load in loads:
+             for i, (s, d) in enumerate(((pot_h, pot), (eps_h, eps), (chg_h, chg), (lab_h, lab), (pat_h, pat), (blk_h, blk)))]
+    for load in loads[:5]:
         load.start()
 
     def at(axis, index):
@@ -111,6 +111,7 @@
 
     loads[0].wait()
     loads[1].wait()
+    loads[5].start()
     def pack1(z, acc):
         acc = jnp.where(pair == z, pltpu.roll(ends(pot[slab(z), :]), 2 * z + 1, 1), acc)
         return jnp.where(pair == z + 32, pltpu.roll(ends(eps[slab(z), :]), 2 * z + 65, 1), acc)
@@ -224,16 +225,26 @@
         return fz_prev
     lax.fori_loop(0, CZ, residual_local, zero)
 
-    loads[4].wait()
+    loads[5].wait()
     def split_blocks(zc, c):
         for xc in range(CX):
             at_block = (zc * CX + xc) * 2
             both = jnp.concatenate([blk[at_block], blk[at_block + 1]], axis=1)
             high, low = split2(both)
-            weights[zc, xc * A:(xc + 1) * A, 0:2 * A] = high
-            weights[zc, xc * A:(xc + 1) * A, 2 * A:4 * A] = low
+            here = pl.ds(pl.multiple_of(zc * A, A), A)
+            weights[xc, here, 0:2 * A] = high
+            weights[xc, here, 2 * A:4 * A] = low
         return c
     lax.fori_loop(0, CZ, split_blocks, 0)
+
+    loads[4].wait()
+    diagonal = lax.broadcasted_iota(jnp.int32, (CZ, CZ), 0) == lax.broadcasted_iota(jnp.int32, (CZ, CZ), 1)
+    names = lax.broadcasted_iota(jnp.int32, (CZ, n * NC), 1).astype(F32)
+    for k in range(2):
+        for xc in range(CX):
+            wanted = jnp.sum(jnp.where(diagonal, pat[xc, 0, k:k + 1, :].astype(F32), 0.0), axis=1, keepdims=True)
+            at_row = (k * CX + xc) * CZ
+            choose[at_row:at_row + CZ, :] = jnp.where(names == wanted, 1.0, 0.0)
 
     merge = jnp.where(lax.broadcasted_iota(jnp.int32, (Y, 128), 0) // 4 == lax.broadcasted_iota(jnp.int32, (Y, 128), 1) % A, 1.0, 0.0).astype(BF16)
 
@@ -284,35 +295,27 @@
     for copy in gathers:
         copy.wait_recv()
 
-    left = lax.broadcasted_iota(jnp.int32, (1, 128), 1) < A
-    for zc in range(CZ):
-        for xc in range(CX):
-            p = jnp.where(left, col[pl.ds(pat[zc, xc, 0, 0], 1), :], col[pl.ds(pat[zc, xc, 0, 1], 1), :])
-            picks[zc * 8 + xc:zc * 8 + xc + 1, :] = p
-            picks[zc * 8 + 4 + xc:zc * 8 + 5 + xc, :] = p
-    half_row = lax.broadcasted_iota(jnp.int32, (8, 128), 0) < 4
-    own_block = (lax.broadcasted_iota(jnp.int32, (8, 4 * A), 0) % 4) == (lax.broadcasted_iota(jnp.int32, (8, 4 * A), 1) // A)
+    left = lax.broadcasted_iota(jnp.int32, (CZ, 128), 1) < A
+    picked = jnp.dot(choose[...].astype(BF16), jnp.concatenate(split2(col[...]), axis=1), preferred_element_type=F32)
+    zrow = lax.broadcasted_iota(jnp.int32, (CZ, 128), 0)
     rows = []
-    for zc in range(CZ):
-        p = picks[zc * 8:zc * 8 + 8, :]
-        high = p.astype(BF16).astype(F32)
-        lhs = jnp.concatenate([jnp.where(half_row, high, p - high), jnp.where(half_row, high, 0.0)], axis=1).astype(BF16)
-        prod = lax.dot_general(lhs, weights[zc], (((1,), (1,)), ((), ())), preferred_element_type=F32)
-        rows.append(jnp.sum(jnp.where(own_block, prod, 0.0), axis=0, keepdims=True))
+    for xc in range(CX):
+        p0, p1 = picked[xc * CZ:(xc + 1) * CZ, :], picked[(CX + xc) * CZ:(CX + xc + 1) * CZ, :]
+        high, low = [jnp.where(left, p0[:, i:i + 128], p1[:, i:i + 128]) for i in (0, 128)]
+        lhs = jnp.concatenate([jnp.concatenate([high, high], axis=1),
+                               jnp.concatenate([low, jnp.zeros_like(low)], axis=1)], axis=0).astype(BF16)
+        prod = lax.dot_general(lhs, weights[xc], (((1,), (1,)), ((), ())), preferred_element_type=F32)
+        prod = prod[0:CZ, :] + prod[CZ:2 * CZ, :]
+        mine_only = jnp.zeros((CZ, 128), F32)
+        for i in range(CZ // 2):
+            mine_only = jnp.where(zrow // 2 == i, prod[:, i * 128:(i + 1) * 128], mine_only)
+        rows.append(jnp.where(left == (zrow % 2 == 0), mine_only, pltpu.roll(mine_only, A, 1)))
     coupled = jnp.concatenate(rows, axis=0)
 
-    def by_lane(value):
-        parts = [value[xc * CZ:(xc + 1) * CZ, :] for xc in range(CX)]
-        return jnp.concatenate([jnp.where(left, parts[i], parts[i + 1]) for i in range(0, CX, 2)], axis=1)
-
-    correction = COARSE_SCALE * (by_lane(coarse_resid) + coupled) / by_lane(coarse_diag)
+    correction = COARSE_SCALE * (coarse_resid + coupled) / coarse_diag
     for xc in range(CX):
-        corr[:, xc, 0, :] = correction[:, xc * A:(xc + 1) * A]
-    stacked = []
-    for xc in range(CX):
-        part = correction[:, (xc // 2) * 128:(xc // 2) * 128 + 128]
-        stacked.append(jnp.where(left if xc % 2 == 0 else jnp.logical_not(left), part, 0.0))
-    high, low = split2(jnp.concatenate(stacked, axis=0))
+        corr[:, xc, 0, :] = correction[xc * CZ:(xc + 1) * CZ, 0:A]
+    high, low = split2(jnp.where(lax.broadcasted_iota(jnp.int32, (NC, 128), 1) < A, correction, 0.0))
     both = lax.dot_general(jnp.concatenate([high, low], axis=0), merge, (((1,), (1,)), ((), ())), preferred_element_type=F32)
     spread[...] = both[0:NC, :] + both[NC:2 * NC, :]
     quarter = row // 4
@@ -343,7 +346,7 @@
         NC = CZ * CX
         flat = (Z * X, Y)
         whole = pltpu.VMEM(flat, F32)
-        any_spec = pl.BlockSpec(memory_space=pl.ANY)
+        any_spec = pl.BlockSpec(memory_space=pltpu.HBM)
         vmem = pl.BlockSpec(memory_space=pltpu.VMEM)
         n = counts[0]
 
@@ -354,21 +357,21 @@
         out, corr = pl.pallas_call(
             functools.partial(kernel, counts, Z, X, Y, A),
             out_shape=(jax.ShapeDtypeStruct(flat, F32), jax.ShapeDtypeStruct((CZ, CX, 1, A), F32)),
-            in_specs=[pl.BlockSpec(memory_space=pltpu.SMEM)] + [any_spec] * 5,
+            in_specs=[any_spec] * 6,
             out_specs=(vmem, vmem),
             scratch_shapes=[
-                whole, whole, whole, pltpu.VMEM(flat, jnp.int32), pltpu.VMEM((2 * NC, A, A), F32),
+                pltpu.VMEM((CX, 1, 2, CZ), jnp.int32), whole, whole, whole, pltpu.VMEM(flat, jnp.int32), pltpu.VMEM((2 * NC, A, A), F32),
                 whole, whole, whole, whole, whole, whole,
                 *halo_scratch(2), *halo_scratch(1),
                 pltpu.VMEM((4 * Z, Y), F32), pltpu.VMEM((CZ * X, Y), F32), pltpu.VMEM((CZ * X, Y), F32),
-                pltpu.VMEM((CZ, CX * A, 4 * A), BF16), pltpu.VMEM((NC, 128), F32), pltpu.VMEM((n * NC, 128), F32),
-                pltpu.VMEM((8 * CZ, 128), F32), pltpu.VMEM((NC, Y), F32),
-                pltpu.SemaphoreType.DMA((5,)), pltpu.SemaphoreType.DMA((14,)), pltpu.SemaphoreType.DMA((14,)),
+                pltpu.VMEM((CX, CZ * A, 4 * A), BF16), pltpu.VMEM((NC, 128), F32), pltpu.VMEM((n * NC, 128), F32),
+                pltpu.VMEM((2 * NC, n * NC), F32), pltpu.VMEM((NC, Y), F32),
+                pltpu.SemaphoreType.DMA((6,)), pltpu.SemaphoreType.DMA((14,)), pltpu.SemaphoreType.DMA((14,)),
                 pltpu.SemaphoreType.DMA((n,)), pltpu.SemaphoreType.DMA((n,)),
             ],
             compiler_params=pltpu.CompilerParams(
-                collective_id=0, has_side_effects=True, vmem_limit_bytes=32 * 1024 * 1024),
-        )(pattern, potential.reshape(flat), charge.reshape(flat), permittivity.reshape(flat), labels.reshape(flat),
+                collective_id=0, has_side_effects=True, vmem_limit_bytes=63 * 1024 * 1024),
+        )(jnp.transpose(pattern, (1, 2, 3, 0)), potential.reshape(flat), charge.reshape(flat), permittivity.reshape(flat), labels.reshape(flat),
           blocks.reshape(2 * NC, A, A))
         return out.reshape(Z, X, Y), corr
 

time: 27.5 us -> 22.8 us (0.83)
  local copies, waits for them, and re-layouts: 7.94 us -> 3.19 us
    unnamed x13 -> x2, local copies, waits for them, and re-layouts: 7.94 us -> 3.19 us
where the time goes in v2:
time: 22.8 us; the launch traced here: 22.5 us
  Pallas kernels  18.7 us (82%)
  local copies, waits for them, and re-layouts  3.19 us (14%)
  between operations  0.64 us (3%)
    pallas_call x1, Pallas kernels, per_device(): pl.pallas_call(functools.partial(kernel, counts, Z, X, Y, A), out_shape=(...  18.7 us
    unnamed x2, local copies, waits for them, and re-layouts  3.19 us

profile of v2, /device:TPU:0, one launch (start us, length us, event | category | flops | bytes accessed | tf_op | source)
XLA Modules:
  0.0 22.5 jit_solution(15880585912286515372)
XLA Ops:
  0.6 18.7 %shard_map.77 = (f32[512,256]{1,0:T(8,128)}, f32[8,4,1,64]{3,2,1,0:T(1,128)}) custom-call(s32[4,1,2,8]{3,2,1,0:T(2,128)} %bitcast.13, f32[512,256]{1,0:T(8,128)} %bitcast.8, f32[512,256]{1,0:T(8,128)} %bitcast.9, f32[512,256]{1,0:T(8,128)} %bitcast.10, s32[512,256]{1,0:T(8,128)} %bitcast.11, f32[64,64,64]{2,1,0:T(8,128)} %bitcast.7), custom_call_target="tpu_custom_call" | custom-call | tf_op jit(solution)/shard_map/pallas_call | solution.py:357
  19.3 1.9 %copy.10 = f32[32,16,256]{2,1,0:T(8,128)} copy(f32[32,16,256]{2,1,0:T(8,128)} %bitcast.12) | data formatting | bytes 1048576
  21.2 1.3 %copy.11 = f32[8,4,1,64]{3,2,1,0:T(1,128)} copy(f32[8,4,1,64]{3,2,1,0:T(1,128)} %get-tuple-element.9) | data formatting | bytes 16384

commit v3 on v2

--- a/solution.py
+++ b/solution.py
@@ -20,11 +20,11 @@
     return high, (value - high.astype(F32)).astype(BF16)
 
 
-def kernel(counts, Z, X, Y, A, pat_h, pot_h, chg_h, eps_h, lab_h, blk_h, out, corr,
-           pat, pot, chg, eps, lab, blk, num, dia, scr, wxs, wys, swp,
+def kernel(counts, Z, X, Y, A, pat_h, pot_h, chg_h, eps_h, lab_h, blk_h, swp, spread, cor,
+           pat, pot, chg, eps, lab, blk, num, dia, scr, wxs, wys,
            zlo, zhi, xlo, xhi, ylo, yhi, xs_lo, xs_hi, ys,
            zlo2, zhi2, xlo2, xhi2, ylo2, yhi2, xs_lo2, xs_hi2, ys2,
-           fx, zsr, zsd, weights, mine, col, choose, spread,
+           fx, zsr, zsd, weights, mine, col, choose,
            in_sem, send_sem, recv_sem, gsend, grecv):
     ids = [lax.axis_index(name) for name in ("gx", "gy", "gz")]
     CZ, CX = Z // 4, X // 4
@@ -313,27 +313,35 @@
     coupled = jnp.concatenate(rows, axis=0)
 
     correction = COARSE_SCALE * (coarse_resid + coupled) / coarse_diag
-    for xc in range(CX):
-        corr[:, xc, 0, :] = correction[xc * CZ:(xc + 1) * CZ, 0:A]
+    cor[...] = correction
     high, low = split2(jnp.where(lax.broadcasted_iota(jnp.int32, (NC, 128), 1) < A, correction, 0.0))
     both = lax.dot_general(jnp.concatenate([high, low], axis=0), merge, (((1,), (1,)), ((), ())), preferred_element_type=F32)
     spread[...] = both[0:NC, :] + both[NC:2 * NC, :]
-    quarter = row // 4
-
-    def finish(zc, c):
-        add = jnp.zeros((X, Y), F32)
-        for xc in range(CX):
-            add = jnp.where(quarter == xc, spread[pl.ds(xc * CZ + zc, 1), :], add)
-        for dz in range(4):
-            z = zc * 4 + dz
-            out[slab(z), :] = swp[slab(z), :] + add
-        return c
-    lax.fori_loop(0, CZ, finish, 0)
-
     wait_send(halo1)
     wait_send(halo2)
     for copy in gathers:
         copy.wait_send()
+
+
+def finish(Z, X, Y, A, swp, spread, cor, out, corr, stage, small, sem):
+    CZ, CX = Z // 4, X // 4
+    for xc in range(CX):
+        small[:, xc, 0, :] = cor[xc * CZ:(xc + 1) * CZ, 0:A]
+    copies = [pltpu.make_async_copy(small, corr, sem.at[CZ])]
+    copies[0].start()
+    quarter = lax.broadcasted_iota(jnp.int32, (X, Y), 0) // 4
+    for zc in range(CZ):
+        add = jnp.zeros((X, Y), F32)
+        for xc in range(CX):
+            add = jnp.where(quarter == xc, spread[xc * CZ + zc:xc * CZ + zc + 1, :], add)
+        for z in range(zc * 4, zc * 4 + 4):
+            stage[z * X:(z + 1) * X, :] = swp[z * X:(z + 1) * X, :] + add
+        rows = pl.ds(zc * 4 * X, 4 * X)
+        copy = pltpu.make_async_copy(stage.at[rows, :], out.at[rows, :], sem.at[zc])
+        copy.start()
+        copies.append(copy)
+    for copy in copies:
+        copy.wait()
 
 
 def solution(mesh):
@@ -354,25 +362,34 @@
             return [pltpu.VMEM((k * X, Y), F32)] * 2 + [pltpu.VMEM((k * Z, Y), F32)] * 2 + [pltpu.VMEM((X, 128), F32)] * 2 + \
                 [pltpu.VMEM((k * Z, Y), F32)] * 2 + [pltpu.VMEM((X, 128), F32)]
 
-        out, corr = pl.pallas_call(
+        swept, spread, cor = pl.pallas_call(
             functools.partial(kernel, counts, Z, X, Y, A),
-            out_shape=(jax.ShapeDtypeStruct(flat, F32), jax.ShapeDtypeStruct((CZ, CX, 1, A), F32)),
+            out_shape=(whole, pltpu.VMEM((NC, Y), F32), pltpu.VMEM((NC, 128), F32)),
             in_specs=[any_spec] * 6,
-            out_specs=(vmem, vmem),
+            out_specs=(vmem, vmem, vmem),
             scratch_shapes=[
                 pltpu.VMEM((CX, 1, 2, CZ), jnp.int32), whole, whole, whole, pltpu.VMEM(flat, jnp.int32), pltpu.VMEM((2 * NC, A, A), F32),
-                whole, whole, whole, whole, whole, whole,
+                whole, whole, whole, whole, whole,
                 *halo_scratch(2), *halo_scratch(1),
                 pltpu.VMEM((4 * Z, Y), F32), pltpu.VMEM((CZ * X, Y), F32), pltpu.VMEM((CZ * X, Y), F32),
                 pltpu.VMEM((CX, CZ * A, 4 * A), BF16), pltpu.VMEM((NC, 128), F32), pltpu.VMEM((n * NC, 128), F32),
-                pltpu.VMEM((2 * NC, n * NC), F32), pltpu.VMEM((NC, Y), F32),
+                pltpu.VMEM((2 * NC, n * NC), F32),
                 pltpu.SemaphoreType.DMA((6,)), pltpu.SemaphoreType.DMA((14,)), pltpu.SemaphoreType.DMA((14,)),
                 pltpu.SemaphoreType.DMA((n,)), pltpu.SemaphoreType.DMA((n,)),
             ],
             compiler_params=pltpu.CompilerParams(
-                collective_id=0, has_side_effects=True, vmem_limit_bytes=63 * 1024 * 1024),
-        )(jnp.transpose(pattern, (1, 2, 3, 0)), potential.reshape(flat), charge.reshape(flat), permittivity.reshape(flat), labels.reshape(flat),
-          blocks.reshape(2 * NC, A, A))
+                collective_id=0, has_side_effects=True, vmem_limit_bytes=32 * 1024 * 1024),
+        )(*[pltpu.with_memory_space_constraint(x, pltpu.HBM) for x in (
+            jnp.transpose(pattern, (1, 2, 3, 0)), potential.reshape(flat), charge.reshape(flat), permittivity.reshape(flat),
+            labels.reshape(flat), blocks.reshape(2 * NC, A, A))])
+        out, corr = pl.pallas_call(
+            functools.partial(finish, Z, X, Y, A),
+            out_shape=(jax.ShapeDtypeStruct(flat, F32), jax.ShapeDtypeStruct((CZ, CX, 1, A), F32)),
+            in_specs=[vmem] * 3,
+            out_specs=(any_spec, any_spec),
+            scratch_shapes=[whole, pltpu.VMEM((CZ, CX, 1, A), F32), pltpu.SemaphoreType.DMA((CZ + 1,))],
+            compiler_params=pltpu.CompilerParams(vmem_limit_bytes=32 * 1024 * 1024),
+        )(swept, spread, cor)
         return out.reshape(Z, X, Y), corr
 
     return jax.shard_map(

time: 22.8 us -> 19.4 us (0.85)
  local copies, waits for them, and re-layouts: 3.19 us -> 0 us
    unnamed x2 -> x0, local copies, waits for them, and re-layouts: 3.19 us -> none
    pallas_call x1, Pallas kernels: 18.7 us -> 17.8 us  [per_device(): pl.pallas_call(functools.partial(kernel, counts, Z, X, Y, A), out_shape=(...]
    pallas_call x0 -> x1, Pallas kernels: none -> 0.88 us  [per_device(): pl.pallas_call(functools.partial(finish, Z, X, Y, A), out_shape=(jax.Shap...]
where the time goes in v3:
time: 19.4 us; the launch traced here: 19.3 us
  Pallas kernels  18.7 us (96%)
  between operations  0.64 us (3%)
    pallas_call x1, Pallas kernels, per_device(): pl.pallas_call(functools.partial(kernel, counts, Z, X, Y, A), out_shape=(...  17.8 us
    pallas_call x1, Pallas kernels, per_device(): pl.pallas_call(functools.partial(finish, Z, X, Y, A), out_shape=(jax.Shap...  0.88 us

profile of v3, /device:TPU:0, one launch (start us, length us, event | category | flops | bytes accessed | tf_op | source)
XLA Modules:
  0.0 19.3 jit_solution(4861037177712342353)
XLA Ops:
  0.6 17.8 %shard_map.77 = (f32[512,256]{1,0:T(8,128)S(1)}, f32[32,256]{1,0:T(8,128)S(1)}, f32[32,128]{1,0:T(8,128)S(1)}) custom-call(s32[4,1,2,8]{3,2,1,0:T(2,128)} %bitcast.12, f32[512,256]{1,0:T(8,128)} %bitcast.8, f32[512,256]{1,0:T(8,128)} %bitcast.9, f32[512,256]{1,0:T(8,128)} %bitcast.10, s32[512,256]{1,0:T(8,128)} %bitcast.11, f32[64,64,64]{2,1,0:T(8,128)} %bitcast.7), custom_call_target="tpu_custom_call" | custom-call | tf_op jit(solution)/shard_map/pallas_call | solution.py:365
  18.4 0.9 %shard_map.78 = (f32[512,256]{1,0:T(8,128)}, f32[8,4,1,64]{3,2,1,0:T(1,128)}) custom-call(f32[512,256]{1,0:T(8,128)S(1)} %get-tuple-element.7.swp, f32[32,256]{1,0:T(8,128)S(1)} %get-tuple-element.8.spread, f32[32,128]{1,0:T(8,128)S(1)} %get-tuple-element.9.cor), custom_call_target="tpu_custom_call" | custom-call | tf_op jit(solution)/shard_map/pallas_call | solution.py:385

commit v4 on v3

--- a/solution.py
+++ b/solution.py
@@ -23,8 +23,7 @@
 def kernel(counts, Z, X, Y, A, pat_h, pot_h, chg_h, eps_h, lab_h, blk_h, swp, spread, cor,
            pat, pot, chg, eps, lab, blk, num, dia, scr, wxs, wys,
            zlo, zhi, xlo, xhi, ylo, yhi, xs_lo, xs_hi, ys,
-           zlo2, zhi2, xlo2, xhi2, ylo2, yhi2, xs_lo2, xs_hi2, ys2,
-           fx, zsr, zsd, weights, mine, col, choose,
+           xs_lo2, xs_hi2, fx, zsr, zsd, weights, mine, zsend_lo, zsend_hi, ysend, col, parts, zin_lo, zin_hi, yin_lo, yin_hi, choose,
            in_sem, send_sem, recv_sem, gsend, grecv):
     ids = [lax.axis_index(name) for name in ("gx", "gy", "gz")]
     CZ, CX = Z // 4, X // 4
@@ -47,19 +46,26 @@
 
     barrier = pltpu.get_barrier_semaphore()
     n = counts[0]
+
+    def peer(d, axis=0, step=0):
+        target = list(ids)
+        if axis:
+            target[axis] = jnp.clip(ids[axis] + step, 0, counts[axis] - 1)
+        target[0] = lax.rem(ids[0] + d, n)
+        return tuple(target)
+
     for d in range(1, n):
-        pl.semaphore_signal(barrier, inc=1, device_id=at(0, lax.rem(ids[0] + d, n)), device_id_type=MESH)
+        pl.semaphore_signal(barrier, inc=1, device_id=peer(d), device_id_type=MESH)
     expected = n - 1
     for axis in (1, 2):
         for ok, step in ((low_ok(axis), -1), (high_ok(axis), 1)):
-            target = jnp.clip(ids[axis] + step, 0, counts[axis] - 1)
-
             @pl.when(ok)
-            def _(target=target, axis=axis):
-                pl.semaphore_signal(barrier, inc=1, device_id=at(axis, target), device_id_type=MESH)
-            expected = expected + ok.astype(jnp.int32)
-
-    for axis, lo_bufs, hi_bufs in ((2, (zlo, zlo2), (zhi, zhi2)), (0, (xlo, xlo2), (xhi, xhi2)), (1, (ylo, ylo2), (yhi, yhi2))):
+            def _(axis=axis, step=step):
+                for d in range(n):
+                    pl.semaphore_signal(barrier, inc=1, device_id=peer(d, axis, step), device_id_type=MESH)
+            expected = expected + n * ok.astype(jnp.int32)
+
+    for axis, lo_bufs, hi_bufs in ((2, (zlo, zin_lo), (zhi, zin_hi)), (0, (xlo,), (xhi,)), (1, (ylo, yin_lo), (yhi, yin_hi))):
         @pl.when(jnp.logical_not(low_ok(axis)))
         def _(bufs=lo_bufs):
             for b in bufs:
@@ -112,10 +118,6 @@
     loads[0].wait()
     loads[1].wait()
     loads[5].start()
-    def pack1(z, acc):
-        acc = jnp.where(pair == z, pltpu.roll(ends(pot[slab(z), :]), 2 * z + 1, 1), acc)
-        return jnp.where(pair == z + 32, pltpu.roll(ends(eps[slab(z), :]), 2 * z + 65, 1), acc)
-    ys[...] = lax.fori_loop(0, Z, pack1, jnp.zeros((X, 128), F32), unroll=8)
     for z in range(Z):
         for k, field in enumerate((pot, eps)):
             xs_lo[k * Z + z:k * Z + z + 1, :] = field[z * X:z * X + 1, :]
@@ -125,11 +127,16 @@
     last = pl.ds((Z - 1) * X, X)
     halo1 = [
         up(0, xs_hi, xlo, 0), down(0, xs_lo, xhi, 1),
-        up(1, ys, ylo, 2), down(1, ys, yhi, 3),
         up(2, pot.at[last, :], zlo.at[pl.ds(0, X), :], 4), up(2, eps.at[last, :], zlo.at[pl.ds(X, X), :], 5),
         down(2, pot.at[first, :], zhi.at[pl.ds(0, X), :], 6), down(2, eps.at[first, :], zhi.at[pl.ds(X, X), :], 7),
+        up(1, ys, ylo, 2), down(1, ys, yhi, 3),
     ]
-    start(halo1)
+    start(halo1[:6])
+    def pack1(z, acc):
+        acc = jnp.where(pair == z, pltpu.roll(ends(pot[slab(z), :]), 2 * z + 1, 1), acc)
+        return jnp.where(pair == z + 32, pltpu.roll(ends(eps[slab(z), :]), 2 * z + 65, 1), acc)
+    ys[...] = lax.fori_loop(0, Z, pack1, jnp.zeros((X, 128), F32), unroll=8)
+    start(halo1[6:])
     loads[2].wait()
     loads[3].wait()
 
@@ -159,7 +166,7 @@
         dia[slab(z), :] = faces + s * (0.5 * (ep + em))
         return fz, wz
     zero = jnp.zeros((X, Y), F32)
-    lax.fori_loop(0, Z, sweep_local, (zero, zero), unroll=2)
+    lax.fori_loop(0, Z, sweep_local, (zero, zero), unroll=4)
 
     wait_recv(halo1)
     wz_lo = 0.5 * (eps[first, :] + zlo[X:2 * X, :])
@@ -181,6 +188,11 @@
     def at_ends(value):
         return jnp.concatenate([jnp.where(lane == 0, value, 0.0), jnp.where(lane == 127, value, 0.0)], axis=1)
 
+    row8 = lax.broadcasted_iota(jnp.int32, (X // 2, Y), 0)
+
+    def at_rows(low, high):
+        return jnp.concatenate([jnp.where(row8 == 0, low, 0.0), jnp.where(row8 == X // 2 - 1, high, 0.0)], axis=0)
+
     def sweep(zc, acc):
         total = jnp.zeros((X, Y), F32)
         for dz in range(4):
@@ -188,8 +200,8 @@
             shift = lax.rem(128 - 2 * z, 128)
             f = at_ends(pltpu.roll(fy_end, shift, 1))
             w = at_ends(pltpu.roll(wy_end, shift, 1))
-            f = f + jnp.where(row == 0, fx[pl.ds(z, 1), :], 0.0) + jnp.where(row == X - 1, fx[pl.ds(2 * Z + z, 1), :], 0.0)
-            w = w + jnp.where(row == 0, fx[pl.ds(Z + z, 1), :], 0.0) + jnp.where(row == X - 1, fx[pl.ds(3 * Z + z, 1), :], 0.0)
+            f = f + at_rows(fx[pl.ds(z, 1), :], fx[pl.ds(2 * Z + z, 1), :])
+            w = w + at_rows(fx[pl.ds(Z + z, 1), :], fx[pl.ds(3 * Z + z, 1), :])
             d = dia[slab(z), :] + w
             total = total + d
             sw = pot[slab(z), :] + OMEGA * (num[slab(z), :] - f) / d
@@ -199,14 +211,7 @@
             acc = jnp.where(pair == z, pltpu.roll(ends(sw), 2 * z + 1, 1), acc)
         zsd[slab(zc), :] = total
         return acc
-    ys2[...] = lax.fori_loop(0, CZ, sweep, jnp.zeros((X, 128), F32))
-
-    halo2 = [
-        up(0, xs_hi2, xlo2, 8), down(0, xs_lo2, xhi2, 9),
-        up(1, ys2, ylo2, 10), down(1, ys2, yhi2, 11),
-        up(2, swp.at[last, :], zlo2, 12), down(2, swp.at[first, :], zhi2, 13),
-    ]
-    start(halo2)
+    ys2 = lax.fori_loop(0, CZ, sweep, jnp.zeros((X, 128), F32), unroll=4)
 
     def residual_local(zc, fz_prev):
         total = jnp.zeros((X, Y), F32)
@@ -223,7 +228,71 @@
             fz_prev = fz
         zsr[slab(zc), :] = total
         return fz_prev
-    lax.fori_loop(0, CZ, residual_local, zero)
+    lax.fori_loop(0, CZ, residual_local, zero, unroll=2)
+
+    merge = jnp.where(lax.broadcasted_iota(jnp.int32, (Y, 128), 0) // 4 == lax.broadcasted_iota(jnp.int32, (Y, 128), 1) % A, 1.0, 0.0).astype(BF16)
+
+    def coarse_rows(ref):
+        groups = []
+        for xc in range(CX):
+            rows = []
+            for zc in range(CZ):
+                base = zc * X + 4 * xc
+                block = ref[zc * X + (xc // 2) * 8:zc * X + (xc // 2) * 8 + 8, :]
+                rows.append(jnp.sum(block[(xc % 2) * 4:(xc % 2) * 4 + 4, :], axis=0, keepdims=True))
+            groups.append(jnp.concatenate(rows, axis=0))
+        return groups
+
+    def merged(groups):
+        high, low = split2(jnp.concatenate(groups, axis=0))
+        both = jnp.dot(jnp.concatenate([high, low], axis=0), merge, preferred_element_type=F32)
+        return (both[0:high.shape[0], :] + both[high.shape[0]:, :]) * (1.0 / 64.0)
+
+    z_lo, z_hi = wz_lo * swp[first, :], wz_hi * swp[last, :]
+    zsr[0:X, :] = zsr[0:X, :] - z_lo
+    zsr[(CZ - 1) * X:CZ * X, :] = zsr[(CZ - 1) * X:CZ * X, :] - z_hi
+    f = wy_end * pltpu.roll(ys2, 127, 1)
+    f = f + pltpu.roll(f, 126, 1)
+    f = f + pltpu.roll(f, 124, 1)
+    for zc in range(CZ):
+        zsr[zc * X:(zc + 1) * X, :] = zsr[zc * X:(zc + 1) * X, :] - at_ends(pltpu.roll(f, (128 - 8 * zc) % 128, 1))
+    groups = coarse_rows(zsr)
+
+    def sum_rows(value):
+        return jnp.concatenate([jnp.sum(value[i:i + 4, :], axis=0, keepdims=True) for i in range(0, value.shape[0], 4)], axis=0)
+
+    x_lo, x_hi = sum_rows(fx[Z:2 * Z, :] * xs_lo2[...]), sum_rows(fx[3 * Z:4 * Z, :] * xs_hi2[...])
+    groups[0] = groups[0] - x_lo
+    groups[-1] = groups[-1] - x_hi
+    z_sums = jnp.concatenate([sum_rows(z_lo), sum_rows(z_hi)], axis=0)
+    both = merged(groups + [x_lo, x_hi, z_sums, jnp.zeros_like(z_sums)])
+    ROWS = NC + 2 * CZ
+    mine[...] = both[0:ROWS, :]
+    zsend_lo[0:CX, :] = both[ROWS:ROWS + CX, :]
+    zsend_hi[0:CX, :] = both[ROWS + CX:ROWS + 2 * CX, :]
+    ysend[0:CX, :] = sum_rows(f) * (1.0 / 64.0)
+    for ref in (zsend_lo, zsend_hi, ysend):
+        ref[CX:8, :] = jnp.zeros((8 - CX, 128), F32)
+
+    def to_peer(src, dst, lane_of_sem, d, axis, step):
+        return pltpu.make_async_remote_copy(
+            src_ref=src, dst_ref=dst, send_sem=gsend.at[lane_of_sem * n + d], recv_sem=grecv.at[lane_of_sem * n + d],
+            device_id=peer(d, axis, step), device_id_type=MESH)
+
+    at_mine = pl.ds(pl.multiple_of(ids[0] * ROWS, 16), ROWS)
+    at_eight = pl.ds(pl.multiple_of(ids[0] * 8, 8), 8)
+    shares = []
+    for kind, (axis, step, src, dst) in enumerate(((1, 1, ysend, yin_lo), (1, -1, ysend, yin_hi), (2, 1, zsend_hi, zin_lo), (2, -1, zsend_lo, zin_hi))):
+        shares.append((axis, step == 1, [to_peer(src, dst.at[at_eight, :], kind + 1, d, axis, step) for d in range(n)]))
+    gathers = [to_peer(mine, parts.at[at_mine, :], 0, d, 0, 0) for d in range(1, n)]
+    for copy in gathers:
+        copy.start()
+    for axis, upward, copies in shares:
+        @pl.when(high_ok(axis) if upward else low_ok(axis))
+        def _(copies=copies):
+            for copy in copies:
+                copy.start()
+    parts[at_mine, :] = both[0:ROWS, :]
 
     loads[5].wait()
     def split_blocks(zc, c):
@@ -246,54 +315,33 @@
             at_row = (k * CX + xc) * CZ
             choose[at_row:at_row + CZ, :] = jnp.where(names == wanted, 1.0, 0.0)
 
-    merge = jnp.where(lax.broadcasted_iota(jnp.int32, (Y, 128), 0) // 4 == lax.broadcasted_iota(jnp.int32, (Y, 128), 1) % A, 1.0, 0.0).astype(BF16)
-
-    def coarse_rows(ref):
-        groups = []
-        for xc in range(CX):
-            rows = []
-            for zc in range(CZ):
-                base = zc * X + 4 * xc
-                block = ref[zc * X + (xc // 2) * 8:zc * X + (xc // 2) * 8 + 8, :]
-                rows.append(jnp.sum(block[(xc % 2) * 4:(xc % 2) * 4 + 4, :], axis=0, keepdims=True))
-            groups.append(jnp.concatenate(rows, axis=0))
-        return groups
-
-    def merged(groups):
-        high, low = split2(jnp.concatenate(groups, axis=0))
-        both = jnp.dot(jnp.concatenate([high, low], axis=0), merge, preferred_element_type=F32)
-        return (both[0:NC, :] + both[NC:2 * NC, :]) * (1.0 / 64.0)
-
     coarse_diag = merged(coarse_rows(zsd))
 
-    wait_recv(halo2)
-    zsr[0:X, :] = zsr[0:X, :] - wz_lo * (swp[first, :] - zlo2[...])
-    zsr[(CZ - 1) * X:CZ * X, :] = zsr[(CZ - 1) * X:CZ * X, :] - wz_hi * (swp[last, :] - zhi2[...])
-    own_y = pltpu.roll(ys2[...], 127, 1)
-    halo_y = jnp.where(even, ylo2[...], pltpu.roll(yhi2[...], 126, 1))
-    f = wy_end * (own_y - halo_y)
-    f = f + pltpu.roll(f, 126, 1)
-    f = f + pltpu.roll(f, 124, 1)
-    for zc in range(CZ):
-        zsr[zc * X:(zc + 1) * X, :] = zsr[zc * X:(zc + 1) * X, :] - at_ends(pltpu.roll(f, (128 - 8 * zc) % 128, 1))
-    groups = coarse_rows(zsr)
-    for k, (own, halo, xc) in enumerate(((xs_lo2, xlo2, 0), (xs_hi2, xhi2, CX - 1))):
-        f = fx[(2 * k + 1) * Z:(2 * k + 2) * Z, :] * (own[...] - halo[...])
-        groups[xc] = groups[xc] - jnp.concatenate(
-            [jnp.sum(f[4 * zc:4 * zc + 4, :], axis=0, keepdims=True) for zc in range(CZ)], axis=0)
-    coarse_resid = merged(groups)
-    mine[...] = coarse_resid
-    my_rows = pl.ds(pl.multiple_of(ids[0] * NC, NC), NC)
-    gathers = []
-    for d in range(1, n):
-        copy = pltpu.make_async_remote_copy(
-            src_ref=mine, dst_ref=col.at[my_rows, :], send_sem=gsend.at[d - 1], recv_sem=grecv.at[d - 1],
-            device_id=at(0, lax.rem(ids[0] + d, n)), device_id_type=MESH)
-        copy.start()
-        gathers.append(copy)
-    col[my_rows, :] = coarse_resid
     for copy in gathers:
         copy.wait_recv()
+    for axis, upward, copies in shares:
+        @pl.when(low_ok(axis) if upward else high_ok(axis))
+        def _(copies=copies):
+            for copy in copies:
+                copy.wait_recv()
+    sub8 = lax.broadcasted_iota(jnp.int32, (CZ, 128), 0)
+    lane8 = lax.broadcasted_iota(jnp.int32, (CZ, 128), 1)
+    low_lane, high_lane = lane8 == 8 * sub8, lane8 == (8 * sub8 + 127) % 128
+    first_cell, last_cell = lane8 % A == 0, lane8 % A == A - 1
+    for g in range(n):
+        for xc in range(CX):
+            b = parts[g * ROWS + xc * CZ:g * ROWS + (xc + 1) * CZ, :]
+            if xc == 0 and g > 0:
+                b = b + parts[(g - 1) * ROWS + NC + CZ:g * ROWS, :]
+            if xc == CX - 1 and g < n - 1:
+                b = b + parts[(g + 1) * ROWS + NC:(g + 1) * ROWS + NC + CZ, :]
+            here = slice(g * 8 + xc, g * 8 + xc + 1)
+            b = b + jnp.where(sub8 == 0, zin_lo[here, :], 0.0) + jnp.where(sub8 == CZ - 1, zin_hi[here, :], 0.0)
+            from_low = jnp.sum(jnp.where(high_lane, yin_lo[here, :], 0.0), axis=1, keepdims=True)
+            from_high = jnp.sum(jnp.where(low_lane, yin_hi[here, :], 0.0), axis=1, keepdims=True)
+            b = b + jnp.where(first_cell, from_low, 0.0) + jnp.where(last_cell, from_high, 0.0)
+            col[g * NC + xc * CZ:g * NC + (xc + 1) * CZ, :] = b
+    coarse_resid = col[pl.ds(pl.multiple_of(ids[0] * NC, NC), NC), :]
 
     left = lax.broadcasted_iota(jnp.int32, (CZ, 128), 1) < A
     picked = jnp.dot(choose[...].astype(BF16), jnp.concatenate(split2(col[...]), axis=1), preferred_element_type=F32)
@@ -318,9 +366,13 @@
     both = lax.dot_general(jnp.concatenate([high, low], axis=0), merge, (((1,), (1,)), ((), ())), preferred_element_type=F32)
     spread[...] = both[0:NC, :] + both[NC:2 * NC, :]
     wait_send(halo1)
-    wait_send(halo2)
     for copy in gathers:
         copy.wait_send()
+    for axis, upward, copies in shares:
+        @pl.when(high_ok(axis) if upward else low_ok(axis))
+        def _(copies=copies):
+            for copy in copies:
+                copy.wait_send()
 
 
 def finish(Z, X, Y, A, swp, spread, cor, out, corr, stage, small, sem):
@@ -358,10 +410,6 @@
         vmem = pl.BlockSpec(memory_space=pltpu.VMEM)
         n = counts[0]
 
-        def halo_scratch(k):
-            return [pltpu.VMEM((k * X, Y), F32)] * 2 + [pltpu.VMEM((k * Z, Y), F32)] * 2 + [pltpu.VMEM((X, 128), F32)] * 2 + \
-                [pltpu.VMEM((k * Z, Y), F32)] * 2 + [pltpu.VMEM((X, 128), F32)]
-
         swept, spread, cor = pl.pallas_call(
             functools.partial(kernel, counts, Z, X, Y, A),
             out_shape=(whole, pltpu.VMEM((NC, Y), F32), pltpu.VMEM((NC, 128), F32)),
@@ -370,12 +418,15 @@
             scratch_shapes=[
                 pltpu.VMEM((CX, 1, 2, CZ), jnp.int32), whole, whole, whole, pltpu.VMEM(flat, jnp.int32), pltpu.VMEM((2 * NC, A, A), F32),
                 whole, whole, whole, whole, whole,
-                *halo_scratch(2), *halo_scratch(1),
+                *[pltpu.VMEM((2 * X, Y), F32)] * 2, *[pltpu.VMEM((2 * Z, Y), F32)] * 2, *[pltpu.VMEM((X, 128), F32)] * 2,
+                *[pltpu.VMEM((2 * Z, Y), F32)] * 2, pltpu.VMEM((X, 128), F32),
+                *[pltpu.VMEM((Z, Y), F32)] * 2,
                 pltpu.VMEM((4 * Z, Y), F32), pltpu.VMEM((CZ * X, Y), F32), pltpu.VMEM((CZ * X, Y), F32),
-                pltpu.VMEM((CX, CZ * A, 4 * A), BF16), pltpu.VMEM((NC, 128), F32), pltpu.VMEM((n * NC, 128), F32),
+                pltpu.VMEM((CX, CZ * A, 4 * A), BF16), pltpu.VMEM((NC + 2 * CZ, 128), F32), *[pltpu.VMEM((8, 128), F32)] * 3,
+                pltpu.VMEM((n * NC, 128), F32), pltpu.VMEM((n * (NC + 2 * CZ), 128), F32), *[pltpu.VMEM((n * 8, 128), F32)] * 4,
                 pltpu.VMEM((2 * NC, n * NC), F32),
-                pltpu.SemaphoreType.DMA((6,)), pltpu.SemaphoreType.DMA((14,)), pltpu.SemaphoreType.DMA((14,)),
-                pltpu.SemaphoreType.DMA((n,)), pltpu.SemaphoreType.DMA((n,)),
+                pltpu.SemaphoreType.DMA((6,)), pltpu.SemaphoreType.DMA((8,)), pltpu.SemaphoreType.DMA((8,)),
+                pltpu.SemaphoreType.DMA((5 * n,)), pltpu.SemaphoreType.DMA((5 * n,)),
             ],
             compiler_params=pltpu.CompilerParams(
                 collective_id=0, has_side_effects=True, vmem_limit_bytes=32 * 1024 * 1024),

time: 19.4 us -> 18.2 us (0.938)
  Pallas kernels: 18.7 us -> 17.4 us
    pallas_call x1, Pallas kernels: 17.8 us -> 16.5 us  [per_device(): pl.pallas_call(functools.partial(kernel, counts, Z, X, Y, A), out_shape=(...]
where the time goes in v4:
time: 18.2 us; the launch traced here: 18 us
  Pallas kernels  17.4 us (96%)
  between operations  0.64 us (4%)
    pallas_call x1, Pallas kernels, per_device(): pl.pallas_call(functools.partial(kernel, counts, Z, X, Y, A), out_shape=(...  16.5 us
    pallas_call x1, Pallas kernels, per_device(): pl.pallas_call(functools.partial(finish, Z, X, Y, A), out_shape=(jax.Shap...  0.88 us

profile of v4, /device:TPU:0, one launch (start us, length us, event | category | flops | bytes accessed | tf_op | source)
XLA Modules:
  0.0 18.0 jit_solution(879847881825232676)
XLA Ops:
  0.6 16.5 %shard_map.77 = (f32[512,256]{1,0:T(8,128)S(1)}, f32[32,256]{1,0:T(8,128)S(1)}, f32[32,128]{1,0:T(8,128)S(1)}) custom-call(s32[4,1,2,8]{3,2,1,0:T(2,128)} %bitcast.12, f32[512,256]{1,0:T(8,128)} %bitcast.8, f32[512,256]{1,0:T(8,128)} %bitcast.9, f32[512,256]{1,0:T(8,128)} %bitcast.10, s32[512,256]{1,0:T(8,128)} %bitcast.11, f32[64,64,64]{2,1,0:T(8,128)} %bitcast.7), custom_call_target="tpu_custom_call" | custom-call | tf_op jit(solution)/shard_map/pallas_call | solution.py:413
  17.2 0.9 %shard_map.78 = (f32[512,256]{1,0:T(8,128)}, f32[8,4,1,64]{3,2,1,0:T(1,128)}) custom-call(f32[512,256]{1,0:T(8,128)S(1)} %get-tuple-element.7.swp, f32[32,256]{1,0:T(8,128)S(1)} %get-tuple-element.8.spread, f32[32,128]{1,0:T(8,128)S(1)} %get-tuple-element.9.cor), custom_call_target="tpu_custom_call" | custom-call | tf_op jit(solution)/shard_map/pallas_call | solution.py:436

commit v5 on v4

--- a/solution.py
+++ b/solution.py
@@ -61,9 +61,8 @@
         for ok, step in ((low_ok(axis), -1), (high_ok(axis), 1)):
             @pl.when(ok)
             def _(axis=axis, step=step):
-                for d in range(n):
-                    pl.semaphore_signal(barrier, inc=1, device_id=peer(d, axis, step), device_id_type=MESH)
-            expected = expected + n * ok.astype(jnp.int32)
+                pl.semaphore_signal(barrier, inc=1, device_id=peer(0, axis, step), device_id_type=MESH)
+            expected = expected + ok.astype(jnp.int32)
 
     for axis, lo_bufs, hi_bufs in ((2, (zlo, zin_lo), (zhi, zin_hi)), (0, (xlo,), (xhi,)), (1, (ylo, yin_lo), (yhi, yin_hi))):
         @pl.when(jnp.logical_not(low_ok(axis)))
@@ -168,6 +167,27 @@
     zero = jnp.zeros((X, Y), F32)
     lax.fori_loop(0, Z, sweep_local, (zero, zero), unroll=4)
 
+    loads[5].wait()
+    def split_blocks(zc, c):
+        for xc in range(CX):
+            at_block = (zc * CX + xc) * 2
+            both = jnp.concatenate([blk[at_block], blk[at_block + 1]], axis=1)
+            high, low = split2(both)
+            here = pl.ds(pl.multiple_of(zc * A, A), A)
+            weights[xc, here, 0:2 * A] = high
+            weights[xc, here, 2 * A:4 * A] = low
+        return c
+    lax.fori_loop(0, CZ, split_blocks, 0)
+
+    loads[4].wait()
+    diagonal = lax.broadcasted_iota(jnp.int32, (CZ, CZ), 0) == lax.broadcasted_iota(jnp.int32, (CZ, CZ), 1)
+    names = lax.broadcasted_iota(jnp.int32, (CZ, n * NC), 1).astype(F32)
+    for k in range(2):
+        for xc in range(CX):
+            wanted = jnp.sum(jnp.where(diagonal, pat[xc, 0, k:k + 1, :].astype(F32), 0.0), axis=1, keepdims=True)
+            at_row = (k * CX + xc) * CZ
+            choose[at_row:at_row + CZ, :] = jnp.where(names == wanted, 1.0, 0.0)
+
     wait_recv(halo1)
     wz_lo = 0.5 * (eps[first, :] + zlo[X:2 * X, :])
     wz_hi = 0.5 * (eps[last, :] + zhi[X:2 * X, :])
@@ -293,27 +313,6 @@
             for copy in copies:
                 copy.start()
     parts[at_mine, :] = both[0:ROWS, :]
-
-    loads[5].wait()
-    def split_blocks(zc, c):
-        for xc in range(CX):
-            at_block = (zc * CX + xc) * 2
-            both = jnp.concatenate([blk[at_block], blk[at_block + 1]], axis=1)
-            high, low = split2(both)
-            here = pl.ds(pl.multiple_of(zc * A, A), A)
-            weights[xc, here, 0:2 * A] = high
-            weights[xc, here, 2 * A:4 * A] = low
-        return c
-    lax.fori_loop(0, CZ, split_blocks, 0)
-
-    loads[4].wait()
-    diagonal = lax.broadcasted_iota(jnp.int32, (CZ, CZ), 0) == lax.broadcasted_iota(jnp.int32, (CZ, CZ), 1)
-    names = lax.broadcasted_iota(jnp.int32, (CZ, n * NC), 1).astype(F32)
-    for k in range(2):
-        for xc in range(CX):
-            wanted = jnp.sum(jnp.where(diagonal, pat[xc, 0, k:k + 1, :].astype(F32), 0.0), axis=1, keepdims=True)
-            at_row = (k * CX + xc) * CZ
-            choose[at_row:at_row + CZ, :] = jnp.where(names == wanted, 1.0, 0.0)
 
     coarse_diag = merged(coarse_rows(zsd))
 

time: 18.2 us -> 17.2 us (0.945)
  Pallas kernels: 17.4 us -> 16.4 us
    pallas_call x1, Pallas kernels: 16.5 us -> 15.5 us  [per_device(): pl.pallas_call(functools.partial(kernel, counts, Z, X, Y, A), out_shape=(...]
where the time goes in v5:
time: 17.2 us; the launch traced here: 17.1 us
  Pallas kernels  16.4 us (95%)
  between operations  0.64 us (4%)
    pallas_call x1, Pallas kernels, per_device(): pl.pallas_call(functools.partial(kernel, counts, Z, X, Y, A), out_shape=(...  15.5 us
    pallas_call x1, Pallas kernels, per_device(): pl.pallas_call(functools.partial(finish, Z, X, Y, A), out_shape=(jax.Shap...  0.88 us

profile of v5, /device:TPU:0, one launch (start us, length us, event | category | flops | bytes accessed | tf_op | source)
XLA Modules:
  0.0 17.1 jit_solution(3272798982440612820)
XLA Ops:
  0.6 15.5 %shard_map.77 = (f32[512,256]{1,0:T(8,128)S(1)}, f32[32,256]{1,0:T(8,128)S(1)}, f32[32,128]{1,0:T(8,128)S(1)}) custom-call(s32[4,1,2,8]{3,2,1,0:T(2,128)} %bitcast.12, f32[512,256]{1,0:T(8,128)} %bitcast.8, f32[512,256]{1,0:T(8,128)} %bitcast.9, f32[512,256]{1,0:T(8,128)} %bitcast.10, s32[512,256]{1,0:T(8,128)} %bitcast.11, f32[64,64,64]{2,1,0:T(8,128)} %bitcast.7), custom_call_target="tpu_custom_call" | custom-call | tf_op jit(solution)/shard_map/pallas_call | solution.py:412
  16.2 0.9 %shard_map.78 = (f32[512,256]{1,0:T(8,128)}, f32[8,4,1,64]{3,2,1,0:T(1,128)}) custom-call(f32[512,256]{1,0:T(8,128)S(1)} %get-tuple-element.7.swp, f32[32,256]{1,0:T(8,128)S(1)} %get-tuple-element.8.spread, f32[32,128]{1,0:T(8,128)S(1)} %get-tuple-element.9.cor), custom_call_target="tpu_custom_call" | custom-call | tf_op jit(solution)/shard_map/pallas_call | solution.py:435

commit v6 on v5

--- a/solution.py
+++ b/solution.py
@@ -32,7 +32,7 @@
 
     loads = [pltpu.make_async_copy(s, d, in_sem.at[i])
              for i, (s, d) in enumerate(((pot_h, pot), (eps_h, eps), (chg_h, chg), (lab_h, lab), (pat_h, pat), (blk_h, blk)))]
-    for load in loads[:5]:
+    for load in loads[:2]:
         load.start()
 
     def at(axis, index):
@@ -116,7 +116,8 @@
 
     loads[0].wait()
     loads[1].wait()
-    loads[5].start()
+    for load in loads[2:]:
+        load.start()
     for z in range(Z):
         for k, field in enumerate((pot, eps)):
             xs_lo[k * Z + z:k * Z + z + 1, :] = field[z * X:z * X + 1, :]
@@ -165,7 +166,7 @@
         dia[slab(z), :] = faces + s * (0.5 * (ep + em))
         return fz, wz
     zero = jnp.zeros((X, Y), F32)
-    lax.fori_loop(0, Z, sweep_local, (zero, zero), unroll=4)
+    lax.fori_loop(0, Z, sweep_local, (zero, zero), unroll=8)
 
     loads[5].wait()
     def split_blocks(zc, c):
@@ -231,7 +232,7 @@
             acc = jnp.where(pair == z, pltpu.roll(ends(sw), 2 * z + 1, 1), acc)
         zsd[slab(zc), :] = total
         return acc
-    ys2 = lax.fori_loop(0, CZ, sweep, jnp.zeros((X, 128), F32), unroll=4)
+    ys2 = lax.fori_loop(0, CZ, sweep, jnp.zeros((X, 128), F32), unroll=8)
 
     def residual_local(zc, fz_prev):
         total = jnp.zeros((X, Y), F32)
@@ -248,7 +249,7 @@
             fz_prev = fz
         zsr[slab(zc), :] = total
         return fz_prev
-    lax.fori_loop(0, CZ, residual_local, zero, unroll=2)
+    lax.fori_loop(0, CZ, residual_local, zero, unroll=4)
 
     merge = jnp.where(lax.broadcasted_iota(jnp.int32, (Y, 128), 0) // 4 == lax.broadcasted_iota(jnp.int32, (Y, 128), 1) % A, 1.0, 0.0).astype(BF16)
 

time: 17.2 us -> 16.8 us (0.977)
  Pallas kernels: 16.4 us -> 16.1 us
    pallas_call x1, Pallas kernels: 15.5 us -> 15.2 us  [per_device(): pl.pallas_call(functools.partial(kernel, counts, Z, X, Y, A), out_shape=(...]
where the time goes in v6:
time: 16.8 us; the launch traced here: 16.7 us
  Pallas kernels  16.1 us (96%)
  between operations  0.64 us (4%)
    pallas_call x1, Pallas kernels, per_device(): pl.pallas_call(functools.partial(kernel, counts, Z, X, Y, A), out_shape=(...  15.2 us
    pallas_call x1, Pallas kernels, per_device(): pl.pallas_call(functools.partial(finish, Z, X, Y, A), out_shape=(jax.Shap...  0.88 us

profile of v6, /device:TPU:0, one launch (start us, length us, event | category | flops | bytes accessed | tf_op | source)
XLA Modules:
  0.0 16.7 jit_solution(11158208606277509133)
XLA Ops:
  0.6 15.2 %shard_map.77 = (f32[512,256]{1,0:T(8,128)S(1)}, f32[32,256]{1,0:T(8,128)S(1)}, f32[32,128]{1,0:T(8,128)S(1)}) custom-call(s32[4,1,2,8]{3,2,1,0:T(2,128)} %bitcast.12, f32[512,256]{1,0:T(8,128)} %bitcast.8, f32[512,256]{1,0:T(8,128)} %bitcast.9, f32[512,256]{1,0:T(8,128)} %bitcast.10, s32[512,256]{1,0:T(8,128)} %bitcast.11, f32[64,64,64]{2,1,0:T(8,128)} %bitcast.7), custom_call_target="tpu_custom_call" | custom-call | tf_op jit(solution)/shard_map/pallas_call | solution.py:413
  15.8 0.9 %shard_map.78 = (f32[512,256]{1,0:T(8,128)}, f32[8,4,1,64]{3,2,1,0:T(1,128)}) custom-call(f32[512,256]{1,0:T(8,128)S(1)} %get-tuple-element.7.swp, f32[32,256]{1,0:T(8,128)S(1)} %get-tuple-element.8.spread, f32[32,128]{1,0:T(8,128)S(1)} %get-tuple-element.9.cor), custom_call_target="tpu_custom_call" | custom-call | tf_op jit(solution)/shard_map/pallas_call | solution.py:436
